TPU v7x, 256 devices: a whole 4x4x8 slice. The times are simulated.
256 devices in a mesh: row: 16 (over x_hi, z), col: 16 (over y, x_lo, core).
Axes of the slice: x: 4 (x_hi: 2, x_lo: 2; x = x_hi * 2 + x_lo), y: 4, z: 8, core: 2. Of those that a mesh axis runs over, the one named last changes fastest.
Arguments:
- iterate: float32 [8192, 18432], P('col', 'row'), may hold values from -6 to 6
- inverse: float32 [18432, 18432], P('col', 'row'), may hold values from -0.125 to 0.125
- lower: float32 [], replicated, may hold values from 0.4 to 0.8
Outputs:
- updated: float32 [8192, 18432], P('col', 'row')
All inputs are finite; a program needn't handle non-finite values.
Results may differ from a plain program's by a relative error of at most 0.0001.
Values sent between devices are 32-bit elements; how exact they have to be, the bound alone decides.
No kernel may reach another device: no remote copies, remote signals or barrier semaphores. Data moves between devices by JAX's collectives and lax.ppermute only.
A program may use at most 64 MiB of HBM per device.

v0:
```python
import jax
import jax.numpy as jnp
from jax import lax
from jax.sharding import PartitionSpec as P


def from_root(value, axis, source):
    kept = jnp.where(lax.axis_index(axis) == source, value, 0).astype(value.dtype)
    return lax.psum(kept, axis)


def from_behind(block, axis, distance):
    devices = range(lax.axis_size(axis))
    route = [((i - distance) % len(devices), i) for i in devices]
    return lax.ppermute(block, axis, route)


def coefficients(lower):
    square = lower * lower
    delta = jnp.cbrt(4.0 * (1.0 - square) / (square * square))
    root = jnp.sqrt(1.0 + delta)
    alpha = root + 0.5 * jnp.sqrt(8.0 - 4.0 * delta + 8.0 * (2.0 - square) / (square * root))
    beta = (alpha - 1.0) * (alpha - 1.0) / 4.0
    gamma = alpha + beta - 1.0
    return (beta / gamma, alpha - beta / gamma)


def multiply(left, right):
    return jnp.dot(left, right, precision=lax.Precision.HIGHEST, preferred_element_type=jnp.float32)


def shards(iterate, inverse, lower):
    columns = lax.axis_size("col")
    per_group = lax.axis_size("row") // columns
    here = lax.axis_index("col")
    keep, lean = coefficients(lower)

    def fetch(which, offset):
        return from_root(iterate, "row", which * per_group + offset)

    def section(which, factor):
        total = multiply(fetch(which, 0), factor)
        return total

    product = section(here, inverse)
    following = (here + 1) % columns
    moved = from_behind(inverse, "col", -1)
    product = product + section(following, moved)
    return keep * iterate + lean * product


def solution(mesh):
    placed = (P("col", "row"), P("col", "row"), P())
    return jax.shard_map(
        shards, mesh=mesh, in_specs=placed, out_specs=P("col", "row"), check_vma=False
    )
```

profile of v0, /device:TPU:8, one launch (start us, length us, event | category | flops | bytes accessed | tf_op | source)
XLA Modules:
  0.0 226.7 jit_solution(5808100553286814484)
XLA Ops:
  6.5 0.0 all-reduce.3.cloned.1.call-start
  6.5 0.8 collective-permute-start
  7.4 4.1 %broadcast_select_fusion = (f32[512,1152]{1,0:T(8,128)}, f32[512,1152]{1,0:T(8,128)}) fusion(f32[512,1152]{1,0:T(8,128)} %param.3, pred[]{:T(512)S(6)} %eq.9, pred[]{:T(512)S(6)} %eq.8), kind=kLoop, calls=%fused_computation.3 | loop fusion | flops 1179648 | bytes 7077890 | tf_op jit(solution)/shard_map/jit(_where)/select_n | solution.py:8
  11.5 0.0 all-reduce.3.cloned.1.call-update
  12.4 178.8 %all-reduce.3.cloned.1.call-done = (f32[512,1152]{1,0:T(8,128)}, f32[512,1152]{1,0:T(8,128)}) async-done(((f32[512,1152]{1,0:T(8,128)}, f32[512,1152]{1,0:T(8,128)}), (f32[512,1152]{1,0:T(8,128)}, f32[512,1152]{1,0:T(8,128)})) %all-reduce.3.cloned.1.call-update) | async-done | bytes 4718608 | tf_op jit(solution)/shard_map/psum | solution.py:9
  191.3 0.0 copy-start
  191.3 0.0 copy-start.1
  191.3 13.9 %fusion.2 = f32[512,1152]{1,0:T(8,128)S(1)} fusion(f32[512,1152]{1,0:T(8,128)} %get-tuple-element.5, f32[1152,1152]{1,0:T(8,128)} %param.4), kind=kOutput, calls=%fused_computation.5 | convolution fusion | flops 8153726976 | bytes 10027008 | tf_op jit(solution)/shard_map/dot_general | solution.py:29
  205.2 0.0 collective-permute-done
  205.2 0.0 copy-done
  205.2 0.0 copy-done.1
  205.2 14.7 %fusion.1 = f32[512,1152]{1,0:T(8,128)} fusion(f32[512,1152]{1,0:T(8,128)S(1)} %fusion.2, f32[512,1152]{1,0:T(8,128)S(1)} %copy-done.1, f32[1152,1152]{1,0:T(8,128)} %collective-permute-done, f32[512,1152]{1,0:T(8,128)S(1)} %copy-done, f32[]{:T(128)S(6)} %sub.24, f32[]{:T(128)S(6)} %div.16), kind=kOutput, calls=%fused_computation.2 | convolution fusion | flops 8156086272 | bytes 14745608 | tf_op jit(solution)/shard_map/dot_general | solution.py:29
Async XLA Ops:
  6.5 184.7 %all-reduce.3.cloned.1.call-start = ((), (), s32[]{:S(2)}) async-start(), calls=%async_computation | async-start | bytes 9437184 | tf_op jit(solution)/shard_map/psum | solution.py:9
  6.5 198.6 %collective-permute-start = (f32[1152,1152]{1,0:T(8,128)}, f32[1152,1152]{1,0:T(8,128)}, u32[]{:S(2)}, u32[]{:S(2)}) collective-permute-start(f32[1152,1152]{1,0:T(8,128)} %param.4), channel_id=1, source_target_pairs={{1,0},{2,1},{3,2},{4,3},{5,4},{6,5},{7,6},{8,7},{9,8},{10,9},{11,1... | collective-permute-start | bytes 15925256 | tf_op jit(solution)/shard_map/ppermute | solution.py:15
  191.3 13.9 %copy-start = (f32[512,1152]{1,0:T(8,128)S(1)}, f32[512,1152]{1,0:T(8,128)}, u32[]{:S(2)}) copy-start(f32[512,1152]{1,0:T(8,128)} %param.3) | copy-start | bytes 7077892
  191.3 13.9 %copy-start.1 = (f32[512,1152]{1,0:T(8,128)S(1)}, f32[512,1152]{1,0:T(8,128)}, u32[]{:S(2)}) copy-start(f32[512,1152]{1,0:T(8,128)} %get-tuple-element.6) | copy-start | bytes 7077892
Sparse Core Ops, SparseCore 0:
  11.6 179.6 all-reduce.2
where the time goes:
time: 227 us
  waiting for transfers between devices  179 us (79%)
  matrix products  28.6 us (13%)
  between operations  14.3 us (6%)
  other arithmetic  4.11 us (2%)
    psum x1, waiting for transfers between devices, from_root(): return lax.psum(kept, axis)  179 us
    dot_general x2, matrix products, multiply(): jnp.dot(left, right, precision=lax.Precision.HIGHEST, preferred_element_t...  28.6 us
  transfers between devices with their start and end apart: 2, of which 1 were waited for; matrix products, arithmetic and copies ran while one was open for 8% of the time, Pallas kernels for 0%

commit v1 on v0

v1 whole, which is shorter than its diff:
```python
import functools

import jax
import jax.numpy as jnp
import numpy as np
from jax import lax
from jax.experimental import pallas as pl
from jax.experimental.pallas import tpu as pltpu
from jax.sharding import PartitionSpec as P

BOTH = ("row", "col")
SAME = ((0, 0), (0, 2), (0, -2), (1, 1), (1, -1), (1, -3), (0, 4), (1, 3))
OTHER = ((0, 1), (0, -1), (1, 0), (0, 3), (0, -3), (1, -2), (1, 2), (1, 4))
GROUPS = ((0, 3), (3, 5), (5, 8))


def coefficients(lower):
    square = lower * lower
    delta = jnp.cbrt(4.0 * (1.0 - square) / (square * square))
    root = jnp.sqrt(1.0 + delta)
    alpha = root + 0.5 * jnp.sqrt(8.0 - 4.0 * delta + 8.0 * (2.0 - square) / (square * root))
    beta = (alpha - 1.0) * (alpha - 1.0) / 4.0
    gamma = alpha + beta - 1.0
    return (beta / gamma, alpha - beta / gamma)


class Grid:
    def __init__(self, n, ring):
        self.n, self.ring = n, ring

    def device(self, row, col):
        return row * self.n + col % self.n

    def label(self, row, col):
        ring, z = row // self.ring, row % self.ring
        return (ring ^ (col // self.ring), (z - col) % self.ring)

    def row_of(self, label, col):
        return ((col // self.ring) ^ label[0]) * self.ring + (col + label[1]) % self.ring

    def shift(self, by):
        return [
            (r, (r // self.ring) * self.ring + (r % self.ring + by) % self.ring)
            for r in range(self.n)
        ]

    def swap(self):
        return [(r, (r + self.ring) % self.n) for r in range(self.n)]

    def near(self, label, kind, d):
        return (label[0] ^ kind, (label[1] + d) % self.ring)

    def tables(self):
        out = np.zeros((self.n, self.n, 17), np.int32)
        for row in range(self.n):
            for col in range(self.n):
                mine = self.label(row, col)
                out[row, col, 0] = sum(mine) % 2
                kept = OTHER if sum(mine) % 2 else SAME
                theirs = self.label(row, (col + 1) % self.n)
                sent = SAME if sum(theirs) % 2 else OTHER
                for i in range(8):
                    out[row, col, 1 + i] = slot_of(self.near(mine, *kept[i]))
                    out[row, col, 9 + i] = slot_of(self.near(theirs, *sent[i]))
        return out.reshape(self.n * self.n, 17)


def slot_of(label):
    return label[1]


def spread(x, grid):
    size = x.shape[0] // 8
    total = None
    for k in range(8):
        route = []
        for c in range(grid.n):
            route.append((grid.device(c, c), grid.device(grid.row_of((k & 1, k), c), c)))
            route.append((grid.device(c, c - 1), grid.device(grid.row_of(((k & 1) ^ 1, k), c), c)))
        got = lax.ppermute(x[size * k : size * (k + 1)], BOTH, route)
        total = got if total is None else total + got
    return total


def gather(piece, grid):
    up = lambda v: lax.ppermute(v, "row", grid.shift(-1))
    down = lambda v: lax.ppermute(v, "row", grid.shift(1))
    over = lambda v: lax.ppermute(v, "row", grid.swap())
    p = {(0, 0): piece}
    p[0, 1], p[0, -1], p[1, 0] = up(piece), down(piece), over(piece)
    p[0, 2], p[0, -2], p[1, 1] = up(p[0, 1]), down(p[0, -1]), over(p[0, 1])
    p[0, 3], p[0, -3], p[1, -1] = up(p[0, 2]), down(p[0, -2]), over(p[0, -1])
    p[1, 2], p[1, -2] = up(p[1, 1]), down(p[1, -1])
    p[0, 4], p[1, -3] = up(p[0, 3]), down(p[1, -2])
    p[1, 3], p[1, 4] = up(p[1, 2]), down(p[1, -3])
    return p


def product_body(n, flag, *refs):
    size = refs[0].shape[0]
    own, opp, (high, low, kept, sent, a, b) = refs[:n], refs[n : 2 * n], refs[2 * n :]
    t = flag[0]
    for base, group in ((t * (n * size), own), ((1 - t) * (n * size), opp)):
        for i, ref in enumerate(group):
            at = pl.ds(pl.multiple_of(base + i * size, size), size)
            v = ref[...]
            top = v.astype(jnp.bfloat16)
            a[at, :] = top
            b[at, :] = (v - top.astype(jnp.float32)).astype(jnp.bfloat16)
    width = high.shape[1]
    for lo in range(0, width, 256):
        cols = slice(lo, min(lo + 256, width))
        dot = lambda x, y: jnp.dot(x, y, preferred_element_type=jnp.float32)
        r = dot(a[...], high[:, cols]) + (dot(b[...], high[:, cols]) + dot(a[...], low[:, cols]))
        kept[:, cols] = r[: n * size]
        sent[:, cols] = r[n * size :]


def product(flag, own, opp, high, low):
    n = len(own)
    size, depth = own[0].shape
    width = high.shape[1]
    vmem = pl.BlockSpec(memory_space=pltpu.VMEM)
    shape = jax.ShapeDtypeStruct((n * size, width), jnp.float32)
    return pl.pallas_call(
        functools.partial(product_body, n),
        out_shape=(shape, shape),
        in_specs=[pl.BlockSpec(memory_space=pltpu.SMEM)] + [vmem] * (2 * n + 2),
        out_specs=(vmem, vmem),
        scratch_shapes=[pltpu.VMEM((2 * n * size, depth), jnp.bfloat16)] * 2,
        compiler_params=pltpu.CompilerParams(vmem_limit_bytes=24 << 20),
        cost_estimate=pl.CostEstimate(
            flops=2 * 3 * 2 * n * size * depth * width,
            bytes_accessed=2 * n * size * 4 * (depth + width) + 4 * depth * width,
            transcendentals=0,
        ),
    )(flag, *own, *opp, high, low)


def finish_body(table, factors, x, *refs):
    out = refs[-1]
    half = (len(refs) - 1) // 2
    kept, sent = refs[:half], refs[half:-1]
    keep, lean = factors[0], factors[1]
    size = x.shape[0] // 8
    i = 0
    for ref in kept:
        for lo in range(0, ref.shape[0], size):
            at = pl.ds(pl.multiple_of(table[1 + i] * size, size), size)
            out[at, :] = keep * x[at, :] + lean * ref[lo : lo + size, :]
            i += 1
    i = 0
    for ref in sent:
        for lo in range(0, ref.shape[0], size):
            at = pl.ds(pl.multiple_of(table[9 + i] * size, size), size)
            out[at, :] = out[at, :] + lean * ref[lo : lo + size, :]
            i += 1


def finish(table, factors, x, kept, sent):
    vmem = pl.BlockSpec(memory_space=pltpu.VMEM)
    smem = pl.BlockSpec(memory_space=pltpu.SMEM)
    return pl.pallas_call(
        finish_body,
        out_shape=jax.ShapeDtypeStruct(x.shape, jnp.float32),
        in_specs=[smem, smem] + [vmem] * (1 + len(kept) + len(sent)),
        out_specs=vmem,
        compiler_params=pltpu.CompilerParams(vmem_limit_bytes=24 << 20),
        cost_estimate=pl.CostEstimate(
            flops=5 * x.size, bytes_accessed=16 * x.size, transcendentals=0
        ),
    )(table, factors, x, *kept, *sent)


def shards(grid, iterate, inverse, lower):
    here = lax.axis_index("row") * grid.n + lax.axis_index("col")
    table = lax.dynamic_index_in_dim(jnp.asarray(grid.tables()), here, 0, keepdims=False)
    factors = jnp.stack(coefficients(lower))
    pieces = gather(spread(iterate, grid), grid)
    high = inverse.astype(jnp.bfloat16)
    low = (inverse - lax.reduce_precision(inverse, 8, 7)).astype(jnp.bfloat16)
    back = [((c + 1) % grid.n, c) for c in range(grid.n)]
    kept, sent = [], []
    for lo, hi in GROUPS:
        own, opp = [pieces[k] for k in SAME[lo:hi]], [pieces[k] for k in OTHER[lo:hi]]
        stay, go = product(table, own, opp, high, low)
        kept.append(stay)
        sent.append(lax.ppermute(go, "col", back))
    return finish(table, factors, iterate, kept, sent)


def solution(mesh):
    grid = Grid(mesh.shape["row"], mesh.shape["row"] // 2)
    placed = (P("col", "row"), P("col", "row"), P())
    return jax.shard_map(
        functools.partial(shards, grid),
        mesh=mesh,
        in_specs=placed,
        out_specs=P("col", "row"),
        check_vma=False,
    )
```

time: 227 us -> 144 us (0.63)
  the two profiles are of different devices: /device:TPU:8 before, /device:TPU:1 now
where the time goes in v1:
time: 144 us; the launch traced here: 143 us
  waiting for transfers between devices  66.1 us (46%)
  starting transfers between devices  37.1 us (26%)
  Pallas kernels  21.1 us (15%)
  local copies, waits for them, and re-layouts  15.3 us (11%)
  other arithmetic  2.65 us (2%)
    ppermute x8, waiting for transfers between devices, spread(): got = lax.ppermute(x[size * k:size * (k + 1)], BOTH, route)  42.2 us
    pallas_call x3, Pallas kernels, product(): pl.pallas_call(functools.partial(product_body, n), out_shape=(shape, shap...  17.3 us
    ppermute x6, starting transfers between devices, gather(): up = lambda v: lax.ppermute(v, 'row', grid.shift(-1))  13.8 us
    unnamed x40, local copies, waits for them, and re-layouts  12.7 us
    ppermute x6, waiting for transfers between devices, gather(): down = lambda v: lax.ppermute(v, 'row', grid.shift(1))  10.3 us
    ppermute x3, starting transfers between devices, gather(): over = lambda v: lax.ppermute(v, 'row', grid.swap())  9.13 us
    ppermute x3, waiting for transfers between devices, shards(): sent.append(lax.ppermute(go, 'col', back))  7.96 us
    ppermute x3, starting transfers between devices, shards(): sent.append(lax.ppermute(go, 'col', back))  7.94 us
  transfers between devices with their start and end apart: 26, of which 6 were waited for; matrix products, arithmetic and copies ran while one was open for 2% of the time, Pallas kernels for 12%

profile of v1, /device:TPU:1, one launch (start us, length us, event | category | flops | bytes accessed | tf_op | source)
XLA Modules:
  0.0 143.4 jit_solution(12018847641157268314)
XLA Ops:
  0.0 1.9 %fusion.1 = (f32[64,1152]{1,0:T(8,128)S(1)}, f32[64,1152]{1,0:T(8,128)S(1)}, f32[64,1152]{1,0:T(8,128)S(1)}, f32[64,1152]{1,0:T(8,128)S(1)}, f32[64,1152]{1,0:T(...) fusion(f32[512,1152]{1,0:T(8,128)} %x.1), kind=kLoop, calls=%fused_computation.5 | loop fusion | bytes 4718592 | tf_op jit(solution)/shard_map/slice | solution.py:80
  1.9 0.8 collective-permute-start
  2.7 0.7 collective-permute-start.1
  3.4 0.7 collective-permute-start.2
  4.1 0.7 collective-permute-start.3
  4.8 0.7 collective-permute-start.4
  5.5 0.7 collective-permute-start.5
  6.2 0.7 collective-permute-start.6
  6.9 0.0 collective-permute-done.2
  6.9 1.3 collective-permute-start.7
  8.2 0.0 collective-permute-done.4
  8.2 0.0 collective-permute-done.5
  8.2 42.2 %collective-permute-done.7 = f32[64,1152]{1,0:T(8,128)S(1)} collective-permute-done((f32[64,1152]{1,0:T(8,128)S(1)}, f32[64,1152]{1,0:T(8,128)S(1)}, u32[]{:S(2)}, u32[]{:S(2)}) %collective-permute-start.7) | collective-permute-done | bytes 294944 | tf_op jit(solution)/shard_map/ppermute | solution.py:80
  50.4 0.1 add_add_fusion.refs_0_
  50.6 0.0 copy-start.9
  50.6 0.1 collective-permute-start.10
  50.7 2.7 %collective-permute-start.8 = (f32[64,1152]{1,0:T(8,128)S(1)}, f32[64,1152]{1,0:T(8,128)S(1)}, u32[]{:S(2)}, u32[]{:S(2)}) collective-permute-start(f32[64,1152]{1,0:T(8,128)S(1)} %add_add_fusion.refs_0_), channel_id=1, source_target_pairs={{0,112},{16,0},{32,16},{48,32},{64,48},{80,64},{96,80},{112,96},{1... | collective-permute-start | bytes 884744 | tf_op jit(solution)/shard_map/ppermute | solution.py:86
  53.3 7.5 %collective-permute-done.10.refs_4_ = f32[64,1152]{1,0:T(8,128)S(1)} collective-permute-done((f32[64,1152]{1,0:T(8,128)S(1)}, f32[64,1152]{1,0:T(8,128)S(1)}, u32[]{:S(2)}, u32[]{:S(2)}) %collective-permute-start.10) | collective-permute-done | bytes 294944 | tf_op jit(solution)/shard_map/ppermute | solution.py:87
  60.8 2.9 %collective-permute-start.14 = (f32[64,1152]{1,0:T(8,128)S(1)}, f32[64,1152]{1,0:T(8,128)S(1)}, u32[]{:S(2)}, u32[]{:S(2)}) collective-permute-start(f32[64,1152]{1,0:T(8,128)S(1)} %collective-permute-done.10.refs_4_), channel_id=1, source_target_pairs={{0,128},{16,144},{32,160},{48,176},{64,192},{80,208},{96,224},{112... | collective-permute-start | bytes 884744 | tf_op jit(solution)/shard_map/ppermute | solution.py:88
  63.8 0.0 collective-permute-done.8.refs_3_
  63.8 0.0 collective-permute-start.9
  63.8 3.2 %collective-permute-start.13 = (f32[64,1152]{1,0:T(8,128)S(1)}, f32[64,1152]{1,0:T(8,128)S(1)}, u32[]{:S(2)}, u32[]{:S(2)}) collective-permute-start(f32[64,1152]{1,0:T(8,128)S(1)} %collective-permute-done.8.refs_3_), channel_id=1, source_target_pairs={{0,128},{16,144},{32,160},{48,176},{64,192},{80,208},{96,224},{112... | collective-permute-start | bytes 884744 | tf_op jit(solution)/shard_map/ppermute | solution.py:88
  67.0 0.7 copy-done.17
  67.7 2.8 %collective-permute-done.14.refs_1_ = f32[64,1152]{1,0:T(8,128)S(1)} collective-permute-done((f32[64,1152]{1,0:T(8,128)S(1)}, f32[64,1152]{1,0:T(8,128)S(1)}, u32[]{:S(2)}, u32[]{:S(2)}) %collective-permute-start.14) | collective-permute-done | bytes 294944 | tf_op jit(solution)/shard_map/ppermute | solution.py:88
  70.5 0.7 copy-done.11
  71.2 3.0 %collective-permute-start.12 = (f32[64,1152]{1,0:T(8,128)S(1)}, f32[64,1152]{1,0:T(8,128)}, u32[]{:S(2)}, u32[]{:S(2)}) collective-permute-start(f32[64,1152]{1,0:T(8,128)S(1)} %add_add_fusion.refs_0_), channel_id=1, source_target_pairs={{0,128},{16,144},{32,160},{48,176},{64,192},{80,208},{96,224},{112... | collective-permute-start | bytes 884744 | tf_op jit(solution)/shard_map/ppermute | solution.py:88
  74.2 0.0 collective-permute-start.11
  74.2 0.7 copy-done.15
  74.9 0.0 collective-permute-done.9.refs_1_
  74.9 2.7 %collective-permute-start.15 = (f32[64,1152]{1,0:T(8,128)}, f32[64,1152]{1,0:T(8,128)}, u32[]{:S(2)}, u32[]{:S(2)}) collective-permute-start(f32[64,1152]{1,0:T(8,128)} %collective-permute-done.9.refs_1_), channel_id=1, source_target_pairs={{0,112},{16,0},{32,16},{48,32},{64,48},{80,64},{96,80},{112,96},{1... | collective-permute-start | bytes 884744 | tf_op jit(solution)/shard_map/ppermute | solution.py:86
  77.6 1.5 %collective-permute-start.20 = (f32[64,1152]{1,0:T(8,128)S(1)}, f32[64,1152]{1,0:T(8,128)}, u32[]{:S(2)}, u32[]{:S(2)}) collective-permute-start(f32[64,1152]{1,0:T(8,128)S(1)} %collective-permute-done.13.refs_0_), channel_id=1, source_target_pairs={{0,112},{16,0},{32,16},{48,32},{64,48},{80,64},{96,80},{112,96},{1... | collective-permute-start | bytes 884744 | tf_op jit(solution)/shard_map/ppermute | solution.py:86
  79.1 0.0 collective-permute-start.18
  79.1 2.5 %fusion = (bf16[1152,1152]{1,0:T(8,128)(2,1)S(1)}, bf16[1152,1152]{1,0:T(8,128)(2,1)}) fusion(f32[1152,1152]{1,0:T(8,128)S(1)} %copy-done.19), kind=kLoop, calls=%fused_computation.1 | loop fusion | flops 5308416 | bytes 10616832 | tf_op jit(solution)/shard_map/convert_element_type | solution.py:181
  81.6 0.0 collective-permute-done.15.refs_2_
  81.6 3.4 %collective-permute-start.19 = (f32[64,1152]{1,0:T(8,128)}, f32[64,1152]{1,0:T(8,128)S(1)}, u32[]{:S(2)}, u32[]{:S(2)}) collective-permute-start(f32[64,1152]{1,0:T(8,128)} %collective-permute-done.15.refs_2_), channel_id=1, source_target_pairs={{0,112},{16,0},{32,16},{48,32},{64,48},{80,64},{96,80},{112,96},{1... | collective-permute-start | bytes 884744 | tf_op jit(solution)/shard_map/ppermute | solution.py:86
  85.0 2.8 %collective-permute-done.20.refs_4_ = f32[64,1152]{1,0:T(8,128)} collective-permute-done((f32[64,1152]{1,0:T(8,128)S(1)}, f32[64,1152]{1,0:T(8,128)}, u32[]{:S(2)}, u32[]{:S(2)}) %collective-permute-start.20) | collective-permute-done | bytes 294944 | tf_op jit(solution)/shard_map/ppermute | solution.py:86
  87.8 3.5 %collective-permute-start.21 = (f32[64,1152]{1,0:T(8,128)}, f32[64,1152]{1,0:T(8,128)S(1)}, u32[]{:S(2)}, u32[]{:S(2)}) collective-permute-start(f32[64,1152]{1,0:T(8,128)} %collective-permute-done.20.refs_4_), channel_id=1, source_target_pairs={{0,112},{16,0},{32,16},{48,32},{64,48},{80,64},{96,80},{112,96},{1... | collective-permute-start | bytes 884744 | tf_op jit(solution)/shard_map/ppermute | solution.py:86
  91.3 0.0 collective-permute-done.18.refs_0_
  91.3 0.0 collective-permute-start.22
  91.4 0.7 dynamic-slice_bitcast_fusion.flag.table
  92.0 0.0 collective-permute-done.12.refs_5_
  92.0 0.0 collective-permute-done.11.refs_2_
  92.1 1.7 %copy-done.3 = bf16[1152,1152]{1,0:T(8,128)(2,1)S(1)} copy-done((bf16[1152,1152]{1,0:T(8,128)(2,1)S(1)}, bf16[1152,1152]{1,0:T(8,128)(2,1)}, u32[]{:S(2)}) %copy-start.3) | copy-done | bytes 2654232
  93.8 1.0 copy-done.10
  94.8 1.0 copy-done.16
  95.7 1.0 copy-done.18
  96.7 6.3 %shard_map.46 = (f32[192,1152]{1,0:T(8,128)S(1)}, f32[192,1152]{1,0:T(8,128)}) custom-call(s32[17]{0:T(128)S(1)} %dynamic-slice_bitcast_fusion.flag.table, f32[64,1152]{1,0:T(8,128)S(1)} %copy-done.10, f32[64,1152]{1,0:T(8,128)} %collective-permute-done.9.refs_1_, f32[64,1152]{1,0:T(8,128)} %collective-permute-done.11.refs_2_, f32[64,1152]{1,0:T(8,128)S(1)} %copy-done.18, ...), custom_call_target="tpu_custom_call" | custom-call | flops 3057647616 | bytes 8847360 | tf_op jit(solution)/shard_map/pallas_call | solution.py:125
  103.0 7.0 %collective-permute-start.23 = (f32[192,1152]{1,0:T(8,128)}, f32[192,1152]{1,0:T(8,128)}, u32[]{:S(2)}, u32[]{:S(2)}) collective-permute-start(f32[192,1152]{1,0:T(8,128)} %get-tuple-element.14), channel_id=1, source_target_pairs={{1,0},{2,1},{3,2},{4,3},{5,4},{6,5},{7,6},{8,7},{9,8},{10,9},{11,1... | collective-permute-start | bytes 2654216 | tf_op jit(solution)/shard_map/ppermute | solution.py:188
  110.1 0.0 collective-permute-done.22.refs_5_
  110.1 6.3 %shard_map.48 = (f32[192,1152]{1,0:T(8,128)S(1)}, f32[192,1152]{1,0:T(8,128)}) custom-call(s32[17]{0:T(128)S(1)} %dynamic-slice_bitcast_fusion.flag.table, f32[64,1152]{1,0:T(8,128)} %collective-permute-done.18.refs_0_, f32[64,1152]{1,0:T(8,128)S(1)} %collective-permute-done.19.refs_1_, f32[64,1152]{1,0:T(8,128)S(1)} %collective-permute-done.21.refs_2_, ...), custom_call_target="tpu_custom_call" | custom-call | flops 3057647616 | bytes 8847360 | tf_op jit(solution)/shard_map/pallas_call | solution.py:125
  116.4 1.0 copy-done.5
  117.4 0.3 collective-permute-start.25
  117.7 2.8 %collective-permute-done.16.refs_3_ = f32[64,1152]{1,0:T(8,128)S(1)} collective-permute-done((f32[64,1152]{1,0:T(8,128)}, f32[64,1152]{1,0:T(8,128)S(1)}, u32[]{:S(2)}, u32[]{:S(2)}) %collective-permute-start.16) | collective-permute-done | bytes 294944 | tf_op jit(solution)/shard_map/ppermute | solution.py:87
  120.5 1.7 %copy-done.2 = bf16[1152,1152]{1,0:T(8,128)(2,1)S(1)} copy-done((bf16[1152,1152]{1,0:T(8,128)(2,1)S(1)}, bf16[1152,1152]{1,0:T(8,128)(2,1)}, u32[]{:S(2)}) %copy-start.2) | copy-done | bytes 2654232
  122.3 4.6 %shard_map.47 = (f32[128,1152]{1,0:T(8,128)S(1)}, f32[128,1152]{1,0:T(8,128)}) custom-call(s32[17]{0:T(128)S(1)} %dynamic-slice_bitcast_fusion.flag.table, f32[64,1152]{1,0:T(8,128)S(1)} %copy-done.14, f32[64,1152]{1,0:T(8,128)S(1)} %copy-done.12, f32[64,1152]{1,0:T(8,128)} %collective-permute-done.15.refs_2_, ...), custom_call_target="tpu_custom_call" | custom-call | flops 2038431744 | bytes 7667712 | tf_op jit(solution)/shard_map/pallas_call | solution.py:125
  126.9 0.8 copy-done.7
  127.7 0.7 collective-permute-start.24
  129.3 0.1 pad_maximum_fusion.factors
  129.4 8.0 %collective-permute-done.24.refs_4_ = f32[128,1152]{1,0:T(8,128)} collective-permute-done((f32[128,1152]{1,0:T(8,128)}, f32[128,1152]{1,0:T(8,128)}, u32[]{:S(2)}, u32[]{:S(2)}) %collective-permute-start.24) | collective-permute-done | bytes 589856 | tf_op jit(solution)/shard_map/ppermute | solution.py:188
  137.4 0.0 collective-permute-done.23.refs_3_
  137.4 0.0 collective-permute-done.25.refs_5_
  137.4 1.2 copy-done.6
  138.6 1.1 copy-done.8
  139.6 3.8 %shard_map.49 = f32[512,1152]{1,0:T(8,128)} custom-call(s32[17]{0:T(128)S(1)} %dynamic-slice_bitcast_fusion.flag.table, f32[2]{0:T(128)S(1)} %pad_maximum_fusion.factors, f32[512,1152]{1,0:T(8,128)S(1)} %copy-done, f32[192,1152]{1,0:T(8,128)S(1)} %get-tuple-element.11.refs_0_, f32[128,1152]{1,0:T(8,128)S(1)} %copy-done.8, f32[192,1152]{1,0:T(8,128)S(1)} %copy-done.6, ...), custom_call_target="tpu_custom_call" | custom-call | flops 2949120 | bytes 9437184 | tf_op jit(solution)/shard_map/pallas_call | solution.py:163
  (37 shorter events, 0.1 us)
Async XLA Ops:
  0.0 79.1 %copy-start.19 = (f32[1152,1152]{1,0:T(8,128)S(1)}, f32[1152,1152]{1,0:T(8,128)}, u32[]{:S(2)}) copy-start(f32[1152,1152]{1,0:T(8,128)} %param.5) | copy-start | bytes 15925252
  1.9 3.6 %collective-permute-start = (f32[64,1152]{1,0:T(8,128)S(1)}, f32[64,1152]{1,0:T(8,128)S(1)}, u32[]{:S(2)}, u32[]{:S(2)}) collective-permute-start(f32[64,1152]{1,0:T(8,128)S(1)} %get-tuple-element.25), channel_id=1, source_target_pairs={{0,0},{15,128},{17,17},{16,145},{34,34},{33,162},{51,51},{50,179},... | collective-permute-start | bytes 884744 | tf_op jit(solution)/shard_map/ppermute | solution.py:80
  2.7 3.5 %collective-permute-start.1 = (f32[64,1152]{1,0:T(8,128)S(1)}, f32[64,1152]{1,0:T(8,128)S(1)}, u32[]{:S(2)}, u32[]{:S(2)}) collective-permute-start(f32[64,1152]{1,0:T(8,128)S(1)} %get-tuple-element.19), channel_id=1, source_target_pairs={{0,144},{15,16},{17,161},{16,33},{34,178},{33,50},{51,195},{50,67}... | collective-permute-start | bytes 884744 | tf_op jit(solution)/shard_map/ppermute | solution.py:80
  3.4 3.5 %collective-permute-start.2 = (f32[64,1152]{1,0:T(8,128)S(1)}, f32[64,1152]{1,0:T(8,128)S(1)}, u32[]{:S(2)}, u32[]{:S(2)}) collective-permute-start(f32[64,1152]{1,0:T(8,128)S(1)} %get-tuple-element.24), channel_id=1, source_target_pairs={{0,32},{15,160},{17,49},{16,177},{34,66},{33,194},{51,83},{50,211}... | collective-permute-start | bytes 884744 | tf_op jit(solution)/shard_map/ppermute | solution.py:80
  4.1 4.1 %collective-permute-start.3 = (f32[64,1152]{1,0:T(8,128)S(1)}, f32[64,1152]{1,0:T(8,128)S(1)}, u32[]{:S(2)}, u32[]{:S(2)}) collective-permute-start(f32[64,1152]{1,0:T(8,128)S(1)} %get-tuple-element.23), channel_id=1, source_target_pairs={{0,176},{15,48},{17,193},{16,65},{34,210},{33,82},{51,227},{50,99}... | collective-permute-start | bytes 884744 | tf_op jit(solution)/shard_map/ppermute | solution.py:80
  4.8 3.4 %collective-permute-start.4 = (f32[64,1152]{1,0:T(8,128)S(1)}, f32[64,1152]{1,0:T(8,128)S(1)}, u32[]{:S(2)}, u32[]{:S(2)}) collective-permute-start(f32[64,1152]{1,0:T(8,128)S(1)} %get-tuple-element.22), channel_id=1, source_target_pairs={{0,64},{15,192},{17,81},{16,209},{34,98},{33,226},{51,115},{50,243... | collective-permute-start | bytes 884744 | tf_op jit(solution)/shard_map/ppermute | solution.py:80
  5.5 2.7 %collective-permute-start.5 = (f32[64,1152]{1,0:T(8,128)S(1)}, f32[64,1152]{1,0:T(8,128)S(1)}, u32[]{:S(2)}, u32[]{:S(2)}) collective-permute-start(f32[64,1152]{1,0:T(8,128)S(1)} %get-tuple-element.21), channel_id=1, source_target_pairs={{0,208},{15,80},{17,225},{16,97},{34,242},{33,114},{51,131},{50,3}... | collective-permute-start | bytes 884744 | tf_op jit(solution)/shard_map/ppermute | solution.py:80
  6.2 2.0 %collective-permute-start.6 = (f32[64,1152]{1,0:T(8,128)S(1)}, f32[64,1152]{1,0:T(8,128)S(1)}, u32[]{:S(2)}, u32[]{:S(2)}) collective-permute-start(f32[64,1152]{1,0:T(8,128)S(1)} %get-tuple-element.20), channel_id=1, source_target_pairs={{0,96},{15,224},{17,113},{16,241},{34,2},{33,130},{51,19},{50,147}... | collective-permute-start | bytes 884744 | tf_op jit(solution)/shard_map/ppermute | solution.py:80
  6.9 43.5 %collective-permute-start.7 = (f32[64,1152]{1,0:T(8,128)S(1)}, f32[64,1152]{1,0:T(8,128)S(1)}, u32[]{:S(2)}, u32[]{:S(2)}) collective-permute-start(f32[64,1152]{1,0:T(8,128)S(1)} %get-tuple-element.26), channel_id=1, source_target_pairs={{0,240},{15,112},{17,129},{16,1},{34,146},{33,18},{51,163},{50,35}... | collective-permute-start | bytes 884744 | tf_op jit(solution)/shard_map/ppermute | solution.py:80
  50.6 31.0 %copy-start.9 = (f32[64,1152]{1,0:T(8,128)}, f32[64,1152]{1,0:T(8,128)S(1)}, u32[]{:S(2)}) copy-start(f32[64,1152]{1,0:T(8,128)S(1)} %add_add_fusion.refs_0_) | copy-start | bytes 884740
  50.6 10.3 %collective-permute-start.10 = (f32[64,1152]{1,0:T(8,128)S(1)}, f32[64,1152]{1,0:T(8,128)S(1)}, u32[]{:S(2)}, u32[]{:S(2)}) collective-permute-start(f32[64,1152]{1,0:T(8,128)S(1)} %add_add_fusion.refs_0_), channel_id=1, source_target_pairs={{0,16},{16,32},{32,48},{48,64},{64,80},{80,96},{96,112},{112,0},{1... | collective-permute-start | bytes 884744 | tf_op jit(solution)/shard_map/ppermute | solution.py:87
  50.7 13.1 %collective-permute-start.8 = (f32[64,1152]{1,0:T(8,128)S(1)}, f32[64,1152]{1,0:T(8,128)S(1)}, u32[]{:S(2)}, u32[]{:S(2)}) collective-permute-start(f32[64,1152]{1,0:T(8,128)S(1)} %add_add_fusion.refs_0_), channel_id=1, source_target_pairs={{0,112},{16,0},{32,16},{48,32},{64,48},{80,64},{96,80},{112,96},{1... | collective-permute-start | bytes 884744 | tf_op jit(solution)/shard_map/ppermute | solution.py:86
  60.8 9.6 %collective-permute-start.14 = (f32[64,1152]{1,0:T(8,128)S(1)}, f32[64,1152]{1,0:T(8,128)S(1)}, u32[]{:S(2)}, u32[]{:S(2)}) collective-permute-start(f32[64,1152]{1,0:T(8,128)S(1)} %collective-permute-done.10.refs_4_), channel_id=1, source_target_pairs={{0,128},{16,144},{32,160},{48,176},{64,192},{80,208},{96,224},{112... | collective-permute-start | bytes 884744 | tf_op jit(solution)/shard_map/ppermute | solution.py:88
  63.8 11.1 %collective-permute-start.9 = (f32[64,1152]{1,0:T(8,128)S(1)}, f32[64,1152]{1,0:T(8,128)}, u32[]{:S(2)}, u32[]{:S(2)}) collective-permute-start(f32[64,1152]{1,0:T(8,128)S(1)} %collective-permute-done.8.refs_3_), channel_id=1, source_target_pairs={{0,112},{16,0},{32,16},{48,32},{64,48},{80,64},{96,80},{112,96},{1... | collective-permute-start | bytes 884744 | tf_op jit(solution)/shard_map/ppermute | solution.py:86
  63.8 13.8 %collective-permute-start.13 = (f32[64,1152]{1,0:T(8,128)S(1)}, f32[64,1152]{1,0:T(8,128)S(1)}, u32[]{:S(2)}, u32[]{:S(2)}) collective-permute-start(f32[64,1152]{1,0:T(8,128)S(1)} %collective-permute-done.8.refs_3_), channel_id=1, source_target_pairs={{0,128},{16,144},{32,160},{48,176},{64,192},{80,208},{96,224},{112... | collective-permute-start | bytes 884744 | tf_op jit(solution)/shard_map/ppermute | solution.py:88
  67.0 0.7 copy-start.17
  70.5 8.6 %collective-permute-start.17 = (f32[64,1152]{1,0:T(8,128)S(1)}, f32[64,1152]{1,0:T(8,128)}, u32[]{:S(2)}, u32[]{:S(2)}) collective-permute-start(f32[64,1152]{1,0:T(8,128)S(1)} %collective-permute-done.14.refs_1_), channel_id=1, source_target_pairs={{0,16},{16,32},{32,48},{48,64},{64,80},{80,96},{96,112},{112,0},{1... | collective-permute-start | bytes 884744 | tf_op jit(solution)/shard_map/ppermute | solution.py:87
  70.5 0.7 copy-start.11
  71.2 20.8 %collective-permute-start.12 = (f32[64,1152]{1,0:T(8,128)S(1)}, f32[64,1152]{1,0:T(8,128)}, u32[]{:S(2)}, u32[]{:S(2)}) collective-permute-start(f32[64,1152]{1,0:T(8,128)S(1)} %add_add_fusion.refs_0_), channel_id=1, source_target_pairs={{0,128},{16,144},{32,160},{48,176},{64,192},{80,208},{96,224},{112... | collective-permute-start | bytes 884744 | tf_op jit(solution)/shard_map/ppermute | solution.py:88
  74.2 17.8 %collective-permute-start.11 = (f32[64,1152]{1,0:T(8,128)S(1)}, f32[64,1152]{1,0:T(8,128)}, u32[]{:S(2)}, u32[]{:S(2)}) collective-permute-start(f32[64,1152]{1,0:T(8,128)S(1)} %collective-permute-done.10.refs_4_), channel_id=1, source_target_pairs={{0,16},{16,32},{32,48},{48,64},{64,80},{80,96},{96,112},{112,0},{1... | collective-permute-start | bytes 884744 | tf_op jit(solution)/shard_map/ppermute | solution.py:87
  74.2 0.7 copy-start.15
  74.9 6.7 %collective-permute-start.15 = (f32[64,1152]{1,0:T(8,128)}, f32[64,1152]{1,0:T(8,128)}, u32[]{:S(2)}, u32[]{:S(2)}) collective-permute-start(f32[64,1152]{1,0:T(8,128)} %collective-permute-done.9.refs_1_), channel_id=1, source_target_pairs={{0,112},{16,0},{32,16},{48,32},{64,48},{80,64},{96,80},{112,96},{1... | collective-permute-start | bytes 884744 | tf_op jit(solution)/shard_map/ppermute | solution.py:86
  77.6 3.9 %copy-start.13 = (f32[64,1152]{1,0:T(8,128)}, f32[64,1152]{1,0:T(8,128)S(1)}, u32[]{:S(2)}) copy-start(f32[64,1152]{1,0:T(8,128)S(1)} %collective-permute-done.13.refs_0_) | copy-start | bytes 884740
  77.6 10.2 %collective-permute-start.20 = (f32[64,1152]{1,0:T(8,128)S(1)}, f32[64,1152]{1,0:T(8,128)}, u32[]{:S(2)}, u32[]{:S(2)}) collective-permute-start(f32[64,1152]{1,0:T(8,128)S(1)} %collective-permute-done.13.refs_0_), channel_id=1, source_target_pairs={{0,112},{16,0},{32,16},{48,32},{64,48},{80,64},{96,80},{112,96},{1... | collective-permute-start | bytes 884744 | tf_op jit(solution)/shard_map/ppermute | solution.py:86
  79.1 12.3 %collective-permute-start.18 = (f32[64,1152]{1,0:T(8,128)}, f32[64,1152]{1,0:T(8,128)}, u32[]{:S(2)}, u32[]{:S(2)}) collective-permute-start(f32[64,1152]{1,0:T(8,128)} %collective-permute-done.17.refs_3_), channel_id=1, source_target_pairs={{0,16},{16,32},{32,48},{48,64},{64,80},{80,96},{96,112},{112,0},{1... | collective-permute-start | bytes 884744 | tf_op jit(solution)/shard_map/ppermute | solution.py:87
  81.6 28.5 %copy-start.1 = (bf16[1152,1152]{1,0:T(8,128)(2,1)}, bf16[1152,1152]{1,0:T(8,128)(2,1)S(1)}, u32[]{:S(2)}) copy-start(bf16[1152,1152]{1,0:T(8,128)(2,1)S(1)} %get-tuple-element.17.refs_7_.refs_5_) | copy-start | bytes 7962628
  81.6 28.5 %collective-permute-start.19 = (f32[64,1152]{1,0:T(8,128)}, f32[64,1152]{1,0:T(8,128)S(1)}, u32[]{:S(2)}, u32[]{:S(2)}) collective-permute-start(f32[64,1152]{1,0:T(8,128)} %collective-permute-done.15.refs_2_), channel_id=1, source_target_pairs={{0,112},{16,0},{32,16},{48,32},{64,48},{80,64},{96,80},{112,96},{1... | collective-permute-start | bytes 884744 | tf_op jit(solution)/shard_map/ppermute | solution.py:86
  87.8 22.2 %collective-permute-start.21 = (f32[64,1152]{1,0:T(8,128)}, f32[64,1152]{1,0:T(8,128)S(1)}, u32[]{:S(2)}, u32[]{:S(2)}) collective-permute-start(f32[64,1152]{1,0:T(8,128)} %collective-permute-done.20.refs_4_), channel_id=1, source_target_pairs={{0,112},{16,0},{32,16},{48,32},{64,48},{80,64},{96,80},{112,96},{1... | collective-permute-start | bytes 884744 | tf_op jit(solution)/shard_map/ppermute | solution.py:86
  91.3 18.7 %collective-permute-start.22 = (f32[64,1152]{1,0:T(8,128)}, f32[64,1152]{1,0:T(8,128)S(1)}, u32[]{:S(2)}, u32[]{:S(2)}) collective-permute-start(f32[64,1152]{1,0:T(8,128)} %collective-permute-done.18.refs_0_), channel_id=1, source_target_pairs={{0,16},{16,32},{32,48},{48,64},{64,80},{80,96},{96,112},{112,0},{1... | collective-permute-start | bytes 884744 | tf_op jit(solution)/shard_map/ppermute | solution.py:87
  92.1 1.8 %copy-start.3 = (bf16[1152,1152]{1,0:T(8,128)(2,1)S(1)}, bf16[1152,1152]{1,0:T(8,128)(2,1)}, u32[]{:S(2)}) copy-start(bf16[1152,1152]{1,0:T(8,128)(2,1)} %get-tuple-element.18.refs_6_.refs_4_) | copy-start | bytes 7962628
  93.8 1.0 copy-start.10
  94.8 1.0 copy-start.16
  95.7 1.0 copy-start.18
  103.0 17.5 %copy-start.4 = (bf16[1152,1152]{1,0:T(8,128)(2,1)S(1)}, bf16[1152,1152]{1,0:T(8,128)(2,1)}, u32[]{:S(2)}) copy-start(bf16[1152,1152]{1,0:T(8,128)(2,1)} %get-tuple-element.18.refs_6_.refs_4_) | copy-start | bytes 7962628
  103.0 17.5 %copy-start.12 = (f32[64,1152]{1,0:T(8,128)S(1)}, f32[64,1152]{1,0:T(8,128)}, u32[]{:S(2)}) copy-start(f32[64,1152]{1,0:T(8,128)} %copy-done.11) | copy-start | bytes 884740
  103.0 17.5 %copy-start.14 = (f32[64,1152]{1,0:T(8,128)S(1)}, f32[64,1152]{1,0:T(8,128)}, u32[]{:S(2)}) copy-start(f32[64,1152]{1,0:T(8,128)} %copy-done.13) | copy-start | bytes 884740
  103.0 34.3 %collective-permute-start.23 = (f32[192,1152]{1,0:T(8,128)}, f32[192,1152]{1,0:T(8,128)}, u32[]{:S(2)}, u32[]{:S(2)}) collective-permute-start(f32[192,1152]{1,0:T(8,128)} %get-tuple-element.14), channel_id=1, source_target_pairs={{1,0},{2,1},{3,2},{4,3},{5,4},{6,5},{7,6},{8,7},{9,8},{10,9},{11,1... | collective-permute-start | bytes 2654216 | tf_op jit(solution)/shard_map/ppermute | solution.py:188
  110.0 10.5 %collective-permute-start.16 = (f32[64,1152]{1,0:T(8,128)}, f32[64,1152]{1,0:T(8,128)S(1)}, u32[]{:S(2)}, u32[]{:S(2)}) collective-permute-start(f32[64,1152]{1,0:T(8,128)} %collective-permute-done.11.refs_2_), channel_id=1, source_target_pairs={{0,16},{16,32},{32,48},{48,64},{64,80},{80,96},{96,112},{112,0},{1... | collective-permute-start | bytes 884744 | tf_op jit(solution)/shard_map/ppermute | solution.py:87
  116.4 1.0 copy-start.5
  117.4 20.0 %copy-start = (f32[512,1152]{1,0:T(8,128)S(1)}, f32[512,1152]{1,0:T(8,128)}, u32[]{:S(2)}) copy-start(f32[512,1152]{1,0:T(8,128)} %x.1) | copy-start | bytes 7077892
  117.4 20.0 %collective-permute-start.25 = (f32[192,1152]{1,0:T(8,128)}, f32[192,1152]{1,0:T(8,128)}, u32[]{:S(2)}, u32[]{:S(2)}) collective-permute-start(f32[192,1152]{1,0:T(8,128)} %get-tuple-element.16), channel_id=1, source_target_pairs={{1,0},{2,1},{3,2},{4,3},{5,4},{6,5},{7,6},{8,7},{9,8},{10,9},{11,1... | collective-permute-start | bytes 2654216 | tf_op jit(solution)/shard_map/ppermute | solution.py:188
  120.5 1.8 %copy-start.2 = (bf16[1152,1152]{1,0:T(8,128)(2,1)S(1)}, bf16[1152,1152]{1,0:T(8,128)(2,1)}, u32[]{:S(2)}) copy-start(bf16[1152,1152]{1,0:T(8,128)(2,1)} %copy-done.1) | copy-start | bytes 7962628
  126.9 0.8 copy-start.7
  127.7 9.6 %collective-permute-start.24 = (f32[128,1152]{1,0:T(8,128)}, f32[128,1152]{1,0:T(8,128)}, u32[]{:S(2)}, u32[]{:S(2)}) collective-permute-start(f32[128,1152]{1,0:T(8,128)} %get-tuple-element.15), channel_id=1, source_target_pairs={{1,0},{2,1},{3,2},{4,3},{5,4},{6,5},{7,6},{8,7},{9,8},{10,9},{11,1... | collective-permute-start | bytes 1769480 | tf_op jit(solution)/shard_map/ppermute | solution.py:188
  137.4 1.2 copy-start.6
  138.6 1.1 copy-start.8

commit v2 on v1

v2 whole, which is shorter than its diff:
```python
import functools

import jax
import jax.numpy as jnp
import numpy as np
from jax import lax
from jax.experimental import pallas as pl
from jax.experimental.pallas import tpu as pltpu
from jax.sharding import PartitionSpec as P

BOTH = ("row", "col")
SAME = ((0, 0), (0, 2), (0, -2), (1, 1), (1, -1), (1, -3), (0, 4), (1, 3))
OTHER = ((0, 1), (0, -1), (1, 0), (0, 3), (0, -3), (1, -2), (1, 2), (1, 4))
GROUPS = ((0, 1), (1, 3), (3, 5), (5, 7), (7, 8))
PLAN = {
    (0, 0): (((2, 0), (0, 1)), (((0, 2), (0, 0), (0, 4), (1, 5)), ((0, 6), (1, 1)), ((1, 3), (1, 7)))),
    (0, 1): (((0, 3), (1, 0)), (((0, 0), (1, 5), (1, 1), (0, 4)), ((1, 3), (1, 7)), ((0, 6), (0, 2)))),
    (1, 0): (((2, 0), (0, 1)), (((0, 7), (1, 6), (1, 4), (0, 3)), ((0, 5), (1, 2)), ((1, 0), (0, 1)))),
    (1, 1): (((3, 0), (0, 1)), (((1, 4), (1, 2), (0, 7), (0, 3)), ((0, 1), (1, 6)), ((0, 5), (1, 0)))),
}


def coefficients(lower):
    square = lower * lower
    delta = jnp.cbrt(4.0 * (1.0 - square) / (square * square))
    root = jnp.sqrt(1.0 + delta)
    alpha = root + 0.5 * jnp.sqrt(8.0 - 4.0 * delta + 8.0 * (2.0 - square) / (square * root))
    beta = (alpha - 1.0) * (alpha - 1.0) / 4.0
    gamma = alpha + beta - 1.0
    return (beta / gamma, alpha - beta / gamma)


class Grid:
    def __init__(self, n, ring):
        self.n, self.ring = n, ring

    def device(self, row, col):
        return row * self.n + col % self.n

    def label(self, row, col):
        ring, z = row // self.ring, row % self.ring
        return (ring ^ (col // self.ring), (z - col) % self.ring)

    def row_of(self, label, col):
        return ((col // self.ring) ^ label[0]) * self.ring + (col + label[1]) % self.ring

    def shift(self, by):
        return [
            (r, (r // self.ring) * self.ring + (r % self.ring + by) % self.ring)
            for r in range(self.n)
        ]

    def moved(self, row, col, move):
        x = (row // self.ring * 2 + col // 2 % 2 + move[0]) % 4
        y = (col // 4 + move[1]) % 4
        return (x // 2 * self.ring + row % self.ring, y * 4 + x % 2 * 2 + col % 2)

    def senders(self, block, c):
        root = (c, (c - block) % self.n)
        return [root] + [self.moved(*root, m) for m in PLAN[block, c % 2][0]]

    def swap(self):
        return [(r, (r + self.ring) % self.n) for r in range(self.n)]

    def near(self, label, kind, d):
        return (label[0] ^ kind, (label[1] + d) % self.ring)

    def tables(self):
        out = np.zeros((self.n, self.n, 17), np.int32)
        for row in range(self.n):
            for col in range(self.n):
                mine = self.label(row, col)
                out[row, col, 0] = sum(mine) % 2
                kept = OTHER if sum(mine) % 2 else SAME
                theirs = self.label(row, (col + 1) % self.n)
                sent = SAME if sum(theirs) % 2 else OTHER
                for i in range(8):
                    out[row, col, 1 + i] = slot_of(0, col, self.near(mine, *kept[i]))
                    out[row, col, 9 + i] = slot_of(1, col + 1, self.near(theirs, *sent[i]))
        return out.reshape(self.n * self.n, 17)


def slot_of(block, c, label):
    return [h for holders in PLAN[block, c % 2][1] for h in holders].index(label)


def spread(x, grid):
    size = x.shape[0] // 8
    groups = [(c, b) for c in range(grid.n) for b in range(2)]

    def hop(relay):
        return [
            (grid.device(*grid.senders(b, c)[0]), grid.device(*grid.senders(b, c)[relay]))
            for c, b in groups
        ]

    def deal(who, j):
        return [
            (
                grid.device(*grid.senders(b, c)[s]),
                grid.device(grid.row_of(PLAN[b, c % 2][1][s][j], c), c),
            )
            for c, b in groups
            for s in who
        ]

    held = [lax.ppermute(x[4 * size : 6 * size], BOTH, hop(1)), lax.ppermute(x[6 * size :], BOTH, hop(2))]
    got = [lax.ppermute(x[size * j : size * (j + 1)], BOTH, deal((0,), j)) for j in range(4)]
    both = [held[0][size * j : size * (j + 1)] + held[1][size * j : size * (j + 1)] for j in range(2)]
    got += [lax.ppermute(both[j], BOTH, deal((1, 2), j)) for j in range(2)]
    return functools.reduce(jnp.add, got), both


def after(value, *others):
    return lax.optimization_barrier((value, *others))[0]


def stages(piece, grid, work, back):
    def move(v, route, where, others):
        with jax.named_scope("piece_%d_%d" % where):
            return lax.ppermute(after(v, *others) if others else v, "row", route)

    up = lambda v, where, *o: move(v, grid.shift(-1), where, o)
    down = lambda v, where, *o: move(v, grid.shift(1), where, o)
    over = lambda v, where, *o: move(v, grid.swap(), where, o)
    p = {(0, 0): piece}

    def far(d, *o):
        p[0, d] = (up if d > 0 else down)(p[0, d - 1 if d > 0 else d + 1], (0, d), *o)

    def cross(d, *o):
        p[1, d] = over(p[0, d], (1, d), *o)

    def along(d, *o):
        p[1, d] = (up if 0 < d < 4 else down)(p[1, d - 1 if 0 < d < 4 else (d + 1 if d < 0 else -3)], (1, d), *o)

    far(1), far(-1), cross(0)
    far(2), far(-2), cross(1)
    far(3), far(-3), cross(-1)
    along(2), along(-2)
    far(4), along(-3)
    along(3), along(4)
    for i in range(5):
        back(i, work(i, p))


def product_body(n, flag, *refs):
    size = refs[0].shape[0]
    own, opp, (high, low, kept, sent, f, a, b, arrive, leave) = refs[:n], refs[n : 2 * n], refs[2 * n :]
    t = flag[0]
    loads = []
    for base, group in ((t * (n * size), own), ((1 - t) * (n * size), opp)):
        for i, ref in enumerate(group):
            at = pl.ds(pl.multiple_of(base + i * size, size), size)
            loads.append(pltpu.make_async_copy(ref, f.at[at], arrive.at[len(loads)]))
    for load in loads:
        load.start()
    for load in loads:
        load.wait()
    for lo in range(0, 2 * n * size, size):
        rows = slice(lo, lo + size)
        v = f[rows, :]
        top = v.astype(jnp.bfloat16)
        a[rows, :] = top
        b[rows, :] = (v - top.astype(jnp.float32)).astype(jnp.bfloat16)
    width = high.shape[1]
    for lo in range(0, width, 256):
        cols = slice(lo, min(lo + 256, width))
        dot = lambda x, y: jnp.dot(x, y, preferred_element_type=jnp.float32)
        f[:, cols] = dot(a[...], high[:, cols]) + (dot(b[...], high[:, cols]) + dot(a[...], low[:, cols]))
    stores = [
        pltpu.make_async_copy(f.at[pl.ds(n * size, n * size)], sent, leave.at[0]),
        pltpu.make_async_copy(f.at[pl.ds(0, n * size)], kept, leave.at[1]),
    ]
    for store in stores:
        store.start()
    for store in stores:
        store.wait()


def product(flag, own, opp, high, low):
    n = len(own)
    size, depth = own[0].shape
    width = high.shape[1]
    vmem = pl.BlockSpec(memory_space=pltpu.VMEM)
    free = pl.BlockSpec(memory_space=pl.ANY)
    shape = jax.ShapeDtypeStruct((n * size, width), jnp.float32)
    return pl.pallas_call(
        functools.partial(product_body, n),
        out_shape=(shape, shape),
        in_specs=[pl.BlockSpec(memory_space=pltpu.SMEM)] + [free] * (2 * n) + [vmem] * 2,
        out_specs=(free, free),
        scratch_shapes=[
            pltpu.VMEM((2 * n * size, depth), jnp.float32),
            pltpu.VMEM((2 * n * size, depth), jnp.bfloat16),
            pltpu.VMEM((2 * n * size, depth), jnp.bfloat16),
            pltpu.SemaphoreType.DMA((2 * n,)),
            pltpu.SemaphoreType.DMA((2,)),
        ],
        compiler_params=pltpu.CompilerParams(vmem_limit_bytes=14 << 20),
        cost_estimate=pl.CostEstimate(
            flops=2 * 3 * 2 * n * size * depth * width,
            bytes_accessed=2 * n * size * 4 * (depth + width) + 4 * depth * width,
            transcendentals=0,
        ),
    )(flag, *own, *opp, high, low)


def finish_body(n, table, factors, x, *refs):
    parts, (out, f, g, arrive, leave) = refs[:-5], refs[-5:]
    keep, lean = factors[0], factors[1]
    size = x.shape[0] // 8
    loads, lo = [pltpu.make_async_copy(x, f, arrive.at[0])], 0
    for ref in parts:
        rows = ref.shape[0]
        loads.append(pltpu.make_async_copy(ref, g.at[pl.ds(lo, rows)], arrive.at[len(loads)]))
        lo += rows
    for load in loads:
        load.start()
    for load in loads:
        load.wait()
    for i in range(n):
        at = pl.ds(pl.multiple_of(table[1 + i] * size, size), size)
        held = keep * f[at, :] if i < 8 else f[at, :]
        f[at, :] = held + lean * g[i * size : (i + 1) * size, :]
    store = pltpu.make_async_copy(f, out, leave.at[0])
    store.start()
    store.wait()


def finish(table, factors, x, parts):
    free = pl.BlockSpec(memory_space=pl.ANY)
    smem = pl.BlockSpec(memory_space=pltpu.SMEM)
    rows = sum(p.shape[0] for p in parts)
    return pl.pallas_call(
        functools.partial(finish_body, rows * 8 // x.shape[0]),
        out_shape=jax.ShapeDtypeStruct(x.shape, jnp.float32),
        in_specs=[smem, smem] + [free] * (1 + len(parts)),
        out_specs=free,
        scratch_shapes=[
            pltpu.VMEM(x.shape, jnp.float32),
            pltpu.VMEM((rows, x.shape[1]), jnp.float32),
            pltpu.SemaphoreType.DMA((1 + len(parts),)),
            pltpu.SemaphoreType.DMA((1,)),
        ],
        compiler_params=pltpu.CompilerParams(vmem_limit_bytes=14 << 20),
        cost_estimate=pl.CostEstimate(
            flops=3 * rows * x.shape[1], bytes_accessed=12 * rows * x.shape[1], transcendentals=0
        ),
    )(table, factors, x, *parts)


def last_body(first, table, factors, held, *refs):
    parts, (out, f, arrive, leave) = refs[:-4], refs[-4:]
    size = held.shape[0] // 8
    n = f.shape[0] // size
    at = [pl.ds(pl.multiple_of(table[9 + first + i] * size, size), size) for i in range(n)]
    mine = [pl.ds(i * size, size) for i in range(n)]
    loads = [pltpu.make_async_copy(held.at[at[i]], f.at[mine[i]], arrive.at[i]) for i in range(n)]
    stores = [pltpu.make_async_copy(f.at[mine[i]], out.at[at[i]], leave.at[i]) for i in range(n)]
    for load in loads:
        load.start()
    i = 0
    for part in parts:
        for lo in range(0, part.shape[0], size):
            loads[i].wait()
            f[mine[i], :] = f[mine[i], :] + factors[1] * part[lo : lo + size, :]
            stores[i].start()
            i += 1
    for store in stores:
        store.wait()


def last(first, table, factors, held, parts):
    free = pl.BlockSpec(memory_space=pl.ANY)
    smem = pl.BlockSpec(memory_space=pltpu.SMEM)
    vmem = pl.BlockSpec(memory_space=pltpu.VMEM)
    n = 8 - first
    return pl.pallas_call(
        functools.partial(last_body, first),
        out_shape=jax.ShapeDtypeStruct(held.shape, jnp.float32),
        in_specs=[smem, smem, free] + [vmem] * len(parts),
        out_specs=free,
        input_output_aliases={2: 0},
        scratch_shapes=[
            pltpu.VMEM((held.shape[0] // 8 * n, held.shape[1]), jnp.float32),
            pltpu.SemaphoreType.DMA((n,)),
            pltpu.SemaphoreType.DMA((n,)),
        ],
        compiler_params=pltpu.CompilerParams(vmem_limit_bytes=6 << 20),
    )(table, factors, held, *parts)


def shards(grid, iterate, inverse, lower):
    here = lax.axis_index("row") * grid.n + lax.axis_index("col")
    table = lax.dynamic_index_in_dim(jnp.asarray(grid.tables()), here, 0, keepdims=False)
    factors = jnp.stack(coefficients(lower))
    piece, relayed = spread(iterate, grid)
    inverse = after(inverse, *relayed)
    high = inverse.astype(jnp.bfloat16)
    low = (inverse - lax.reduce_precision(inverse, 8, 7)).astype(jnp.bfloat16)
    piece, high, low, table, factors = lax.optimization_barrier((piece, high, low, table, factors))
    back = [((c + 1) % grid.n, c) for c in range(grid.n)]
    kept, sent = [], []

    def work(i, pieces, *others):
        lo, hi = GROUPS[i]
        own, opp = [pieces[k] for k in SAME[lo:hi]], [pieces[k] for k in OTHER[lo:hi]]
        if others:
            own[0] = after(own[0], *(pieces[k] for k in others))
        if i >= 2:
            own[0], sent[i - 2] = lax.optimization_barrier((own[0], sent[i - 2]))
        stay, go = product(table, own, opp, high, low)
        kept.append(stay)
        return go

    def send(i, go):
        with jax.named_scope("return_%d" % i):
            sent.append(lax.ppermute(go, "col", back))

    stages(piece, grid, work, send)
    early = 3
    out = finish(table, factors, iterate, kept + sent[:early])
    return last(GROUPS[early][0], table, factors, out, sent[early:])


def solution(mesh):
    grid = Grid(mesh.shape["row"], mesh.shape["row"] // 2)
    placed = (P("col", "row"), P("col", "row"), P())
    return jax.shard_map(
        functools.partial(shards, grid),
        mesh=mesh,
        in_specs=placed,
        out_specs=P("col", "row"),
        check_vma=False,
    )
```

time: 144 us -> 105 us (0.73)
  waiting for transfers between devices: 66.1 us -> 22.2 us
  local copies, waits for them, and re-layouts: 15.3 us -> 4.24 us
  starting transfers between devices: 37.1 us -> 47.8 us
  other arithmetic: 2.65 us -> 6.36 us
    ppermute x26 -> x28, waiting for transfers between devices: 66.1 us -> 22.2 us  [the longest x15 13.8 us: move(): return lax.ppermute(after(v, *others) if others else v, 'row', route)]
    unnamed x40 -> x2, local copies, waits for them, and re-layouts: 12.7 us -> 0.01 us
    ppermute x26 -> x28, starting transfers between devices: 37.1 us -> 47.8 us  [the longest x15 33.4 us: move(): return lax.ppermute(after(v, *others) if others else v, 'row', route)]
    convert_element_type x1, other arithmetic: 2.46 us -> 4.96 us  [shards(): low = (inverse - lax.reduce_precision(inverse, 8, 7)).astype(jnp.bfloat16)]
    pallas_call x1 -> x2, Pallas kernels: 3.76 us -> 6.17 us  [the longest x1 3.65 us: finish(): pl.pallas_call(functools.partial(finish_body, rows * 8 // x.shape[0]), ou...]
    slice x1 -> x2, local copies, waits for them, and re-layouts: 1.91 us -> 3.53 us  [the longest x1 2.47 us: spread(): x[4 * size:6 * size]]
    pallas_call x3 -> x5, Pallas kernels: 17.3 us -> 16.2 us  [product(): pl.pallas_call(functools.partial(product_body, n), out_shape=(shape, shap...]
  transfers between devices with their start and end apart: 26 -> 28, of which waited for: 6 -> 9; matrix products, arithmetic and copies ran while one was open for 2% -> 7% of each run, Pallas kernels for 12% -> 19%
where the time goes in v2:
time: 105 us; the launch traced here: 104 us
  starting transfers between devices  47.8 us (46%)
  Pallas kernels  22.3 us (21%)
  waiting for transfers between devices  22.2 us (21%)
  other arithmetic  6.36 us (6%)
  local copies, waits for them, and re-layouts  4.24 us (4%)
  between operations  1.29 us (1%)
    ppermute x15, starting transfers between devices, move(): return lax.ppermute(after(v, *others) if others else v, 'row', route)  33.4 us
    pallas_call x5, Pallas kernels, product(): pl.pallas_call(functools.partial(product_body, n), out_shape=(shape, shap...  16.2 us
    ppermute x15, waiting for transfers between devices, move(): return lax.ppermute(after(v, *others) if others else v, 'row', route)  13.8 us
    ppermute x5, starting transfers between devices, send(): sent.append(lax.ppermute(go, 'col', back))  6.9 us
    ppermute x4, waiting for transfers between devices, spread(): lax.ppermute(x[size * j:size * (j + 1)], BOTH, deal((0,), j))  5.69 us
    convert_element_type x1, other arithmetic, shards(): low = (inverse - lax.reduce_precision(inverse, 8, 7)).astype(jnp.bfloat16)  4.96 us
    ppermute x4, starting transfers between devices, spread(): lax.ppermute(x[size * j:size * (j + 1)], BOTH, deal((0,), j))  4.71 us
    pallas_call x1, Pallas kernels, finish(): pl.pallas_call(functools.partial(finish_body, rows * 8 // x.shape[0]), ou...  3.65 us
  transfers between devices with their start and end apart: 28, of which 9 were waited for; matrix products, arithmetic and copies ran while one was open for 7% of the time, Pallas kernels for 19%

profile of v2, /device:TPU:1, one launch (start us, length us, event | category | flops | bytes accessed | tf_op | source)
XLA Modules:
  0.0 104.2 jit_solution(14116710525446447345)
XLA Ops:
  0.0 2.5 %fusion.2 = (f32[128,1152]{1,0:T(8,128)}, f32[128,1152]{1,0:T(8,128)}) fusion(f32[512,1152]{1,0:T(8,128)} %x.1), kind=kLoop, calls=%fused_computation.8 | loop fusion | bytes 2359296 | tf_op jit(solution)/shard_map/slice | solution.py:107
  2.5 0.7 collective-permute-start.5
  3.2 0.7 collective-permute-start.4
  3.9 1.1 %fusion.1 = (f32[64,1152]{1,0:T(8,128)}, f32[64,1152]{1,0:T(8,128)}, f32[64,1152]{1,0:T(8,128)}, f32[64,1152]{1,0:T(8,128)}) fusion(f32[512,1152]{1,0:T(8,128)S(1)} %copy-done), kind=kLoop, calls=%fused_computation.7 | loop fusion | bytes 2359296 | tf_op jit(solution)/shard_map/slice | solution.py:108
  4.9 1.4 %collective-permute-start.3 = (f32[64,1152]{1,0:T(8,128)}, f32[64,1152]{1,0:T(8,128)}, u32[]{:S(2)}, u32[]{:S(2)}) collective-permute-start(f32[64,1152]{1,0:T(8,128)} %get-tuple-element.52), channel_id=1, source_target_pairs={{0,208},{15,48},{17,81},{16,65},{34,242},{33,82},{51,115},{50,99},... | collective-permute-start | bytes 884744 | tf_op jit(solution)/shard_map/ppermute | solution.py:108
  6.3 1.3 %collective-permute-start.2 = (f32[64,1152]{1,0:T(8,128)}, f32[64,1152]{1,0:T(8,128)}, u32[]{:S(2)}, u32[]{:S(2)}) collective-permute-start(f32[64,1152]{1,0:T(8,128)} %get-tuple-element.53), channel_id=1, source_target_pairs={{0,64},{15,192},{17,161},{16,1},{34,98},{33,226},{51,195},{50,35},... | collective-permute-start | bytes 884744 | tf_op jit(solution)/shard_map/ppermute | solution.py:108
  7.6 1.4 %collective-permute-start = (f32[64,1152]{1,0:T(8,128)}, f32[64,1152]{1,0:T(8,128)}, u32[]{:S(2)}, u32[]{:S(2)}) collective-permute-start(f32[64,1152]{1,0:T(8,128)} %get-tuple-element.54), channel_id=1, source_target_pairs={{0,32},{15,112},{17,17},{16,209},{34,66},{33,18},{51,51},{50,243},... | collective-permute-start | bytes 884744 | tf_op jit(solution)/shard_map/ppermute | solution.py:108
  9.9 0.7 dynamic-slice_bitcast_fusion.flag.table
  10.6 0.1 pad_maximum_fusion.factors
  10.7 0.0 collective-permute-done.5
  10.7 0.7 collective-permute-start.1
  11.4 0.0 collective-permute-done.4
  11.4 0.1 slice_add_fusion.1
  11.5 0.7 collective-permute-start.7
  12.1 0.0 collective-permute-done.3
  12.2 0.7 collective-permute-start.6
  12.8 5.0 %fusion = (bf16[1152,1152]{1,0:T(8,128)(2,1)S(1)}, bf16[1152,1152]{1,0:T(8,128)(2,1)S(1)}) fusion(f32[1152,1152]{1,0:T(8,128)} %param.5), kind=kLoop, calls=%fused_computation.1 | loop fusion | flops 5308416 | bytes 10616832 | tf_op jit(solution)/shard_map/convert_element_type | solution.py:301
  17.8 5.7 %collective-permute-done.2 = f32[64,1152]{1,0:T(8,128)} collective-permute-done((f32[64,1152]{1,0:T(8,128)}, f32[64,1152]{1,0:T(8,128)}, u32[]{:S(2)}, u32[]{:S(2)}) %collective-permute-start.2) | collective-permute-done | bytes 294944 | tf_op jit(solution)/shard_map/ppermute | solution.py:108
  23.5 0.0 collective-permute-done
  23.5 0.0 collective-permute-done.1
  23.5 0.0 collective-permute-done.7
  23.5 0.0 collective-permute-done.6
  23.5 1.3 %add_add_fusion.refs_0_ = f32[64,1152]{1,0:T(8,128)S(1)} fusion(f32[64,1152]{1,0:T(8,128)S(1)} %collective-permute-done.7, f32[64,1152]{1,0:T(8,128)S(1)} %collective-permute-done.6, f32[64,1152]{1,0:T(8,128)} %collective-permute-done.3, f32[64,1152]{1,0:T(8,128)} %collective-permute-done.2, f32[64,1152]{1,0:T(8,128)} %collective-permute-done, ...), kind=kLoop, calls=%fused_computation.4 | loop fusion | flops 368640 | bytes 2064384 | tf_op jit(solution)/shard_map/add | solution.py:111
  24.8 15.3 %collective-permute-start.8 = (f32[64,1152]{1,0:T(8,128)S(1)}, f32[64,1152]{1,0:T(8,128)S(1)}, u32[]{:S(2)}, u32[]{:S(2)}) collective-permute-start(f32[64,1152]{1,0:T(8,128)S(1)} %add_add_fusion.refs_0_), channel_id=1, source_target_pairs={{0,112},{16,0},{32,16},{48,32},{64,48},{80,64},{96,80},{112,96},{1... | collective-permute-start | bytes 884744 | tf_op jit(solution)/shard_map/piece_0_1/ppermute | solution.py:121
  40.1 0.0 collective-permute-start.10
  40.1 0.0 collective-permute-start.12
  40.1 4.2 %collective-permute-done.8.refs_1_ = f32[64,1152]{1,0:T(8,128)S(1)} collective-permute-done((f32[64,1152]{1,0:T(8,128)S(1)}, f32[64,1152]{1,0:T(8,128)S(1)}, u32[]{:S(2)}, u32[]{:S(2)}) %collective-permute-start.8) | collective-permute-done | bytes 294944 | tf_op jit(solution)/shard_map/piece_0_1/ppermute | solution.py:121
  44.3 3.4 %collective-permute-start.9 = (f32[64,1152]{1,0:T(8,128)S(1)}, f32[64,1152]{1,0:T(8,128)S(1)}, u32[]{:S(2)}, u32[]{:S(2)}) collective-permute-start(f32[64,1152]{1,0:T(8,128)S(1)} %collective-permute-done.8.refs_1_), channel_id=1, source_target_pairs={{0,112},{16,0},{32,16},{48,32},{64,48},{80,64},{96,80},{112,96},{1... | collective-permute-start | bytes 884744 | tf_op jit(solution)/shard_map/piece_0_2/ppermute | solution.py:121
  47.7 0.4 collective-permute-done.10.refs_2_
  48.1 0.4 collective-permute-start.11
  48.5 3.0 %collective-permute-start.13 = (f32[64,1152]{1,0:T(8,128)S(1)}, f32[64,1152]{1,0:T(8,128)S(1)}, u32[]{:S(2)}, u32[]{:S(2)}) collective-permute-start(f32[64,1152]{1,0:T(8,128)S(1)} %collective-permute-done.8.refs_1_), channel_id=1, source_target_pairs={{0,128},{16,144},{32,160},{48,176},{64,192},{80,208},{96,224},{112... | collective-permute-start | bytes 884744 | tf_op jit(solution)/shard_map/piece_1_1/ppermute | solution.py:121
  51.5 2.3 %shard_map.46 = (f32[64,1152]{1,0:T(8,128)S(1)}, f32[64,1152]{1,0:T(8,128)S(1)}) custom-call(s32[17]{0:T(128)S(1)} %dynamic-slice_bitcast_fusion.flag.table, f32[64,1152]{1,0:T(8,128)S(1)} %add_add_fusion.refs_0_, f32[64,1152]{1,0:T(8,128)S(1)} %collective-permute-done.8.refs_1_, bf16[1152,1152]{1,0:T(8,128)(2,1)S(1)} %get-tuple-element.31.refs_2_.refs_4_, ...), custom_call_target="tpu_custom_call" | custom-call | flops 1019215872 | bytes 6488064 | tf_op jit(solution)/shard_map/pallas_call | solution.py:188
  53.8 0.8 collective-permute-start.14
  54.6 4.5 %collective-permute-start.16 = (f32[64,1152]{1,0:T(8,128)S(1)}, f32[64,1152]{1,0:T(8,128)S(1)}, u32[]{:S(2)}, u32[]{:S(2)}) collective-permute-start(f32[64,1152]{1,0:T(8,128)S(1)} %collective-permute-done.9.refs_0_), channel_id=1, source_target_pairs={{0,112},{16,0},{32,16},{48,32},{64,48},{80,64},{96,80},{112,96},{1... | collective-permute-start | bytes 884744 | tf_op jit(solution)/shard_map/piece_0_3/ppermute | solution.py:121
  59.1 0.0 collective-permute-done.11.refs_1_
  59.1 0.0 collective-permute-start.17
  59.1 0.0 collective-permute-done.15.refs_1_
  59.1 0.3 collective-permute-start.18
  59.4 3.9 %shard_map.47 = (f32[128,1152]{1,0:T(8,128)S(1)}, f32[128,1152]{1,0:T(8,128)S(1)}) custom-call(s32[17]{0:T(128)S(1)} %dynamic-slice_bitcast_fusion.flag.table, f32[64,1152]{1,0:T(8,128)S(1)} %collective-permute-done.9.refs_0_, f32[64,1152]{1,0:T(8,128)S(1)} %collective-permute-done.11.refs_1_, f32[64,1152]{1,0:T(8,128)S(1)} %collective-permute-done.10.refs_2_, ...), custom_call_target="tpu_custom_call" | custom-call | flops 2038431744 | bytes 7667712 | tf_op jit(solution)/shard_map/pallas_call | solution.py:188
  63.3 1.6 %collective-permute-done.13.refs_0_ = f32[64,1152]{1,0:T(8,128)S(1)} collective-permute-done((f32[64,1152]{1,0:T(8,128)S(1)}, f32[64,1152]{1,0:T(8,128)S(1)}, u32[]{:S(2)}, u32[]{:S(2)}) %collective-permute-start.13) | collective-permute-done | bytes 294944 | tf_op jit(solution)/shard_map/piece_1_1/ppermute | solution.py:121
  64.8 1.0 collective-permute-start.20
  65.8 1.5 %collective-permute-done.14.refs_5_ = f32[64,1152]{1,0:T(8,128)S(1)} collective-permute-done((f32[64,1152]{1,0:T(8,128)S(1)}, f32[64,1152]{1,0:T(8,128)S(1)}, u32[]{:S(2)}, u32[]{:S(2)}) %collective-permute-start.14) | collective-permute-done | bytes 294944 | tf_op jit(solution)/shard_map/return_0/ppermute | solution.py:319
  67.3 2.5 %collective-permute-start.22 = (f32[64,1152]{1,0:T(8,128)S(1)}, f32[64,1152]{1,0:T(8,128)S(1)}, u32[]{:S(2)}, u32[]{:S(2)}) collective-permute-start(f32[64,1152]{1,0:T(8,128)S(1)} %collective-permute-done.13.refs_0_), channel_id=1, source_target_pairs={{0,112},{16,0},{32,16},{48,32},{64,48},{80,64},{96,80},{112,96},{1... | collective-permute-start | bytes 884744 | tf_op jit(solution)/shard_map/piece_1_2/ppermute | solution.py:121
  69.8 5.1 %collective-permute-done.18.refs_2_ = f32[64,1152]{1,0:T(8,128)S(1)} collective-permute-done((f32[64,1152]{1,0:T(8,128)S(1)}, f32[64,1152]{1,0:T(8,128)S(1)}, u32[]{:S(2)}, u32[]{:S(2)}) %collective-permute-start.18) | collective-permute-done | bytes 294944 | tf_op jit(solution)/shard_map/piece_1_-2/ppermute | solution.py:121
  74.9 0.0 collective-permute-start.19
  74.9 0.0 collective-permute-done.16.refs_2_
  74.9 2.7 %collective-permute-start.21 = (f32[64,1152]{1,0:T(8,128)S(1)}, f32[64,1152]{1,0:T(8,128)S(1)}, u32[]{:S(2)}, u32[]{:S(2)}) collective-permute-start(f32[64,1152]{1,0:T(8,128)S(1)} %collective-permute-done.16.refs_2_), channel_id=1, source_target_pairs={{0,112},{16,0},{32,16},{48,32},{64,48},{80,64},{96,80},{112,96},{1... | collective-permute-start | bytes 884744 | tf_op jit(solution)/shard_map/piece_0_4/ppermute | solution.py:121
  77.6 3.8 %shard_map.48 = (f32[128,1152]{1,0:T(8,128)S(1)}, f32[128,1152]{1,0:T(8,128)S(1)}) custom-call(s32[17]{0:T(128)S(1)} %dynamic-slice_bitcast_fusion.flag.table, f32[64,1152]{1,0:T(8,128)S(1)} %collective-permute-done.13.refs_0_, f32[64,1152]{1,0:T(8,128)S(1)} %collective-permute-done.15.refs_1_, f32[64,1152]{1,0:T(8,128)S(1)} %collective-permute-done.16.refs_2_, ...), custom_call_target="tpu_custom_call" | custom-call | flops 2038431744 | bytes 7667712 | tf_op jit(solution)/shard_map/pallas_call | solution.py:188
  81.4 1.8 %collective-permute-start.24 = (f32[128,1152]{1,0:T(8,128)S(1)}, f32[128,1152]{1,0:T(8,128)S(1)}, u32[]{:S(2)}, u32[]{:S(2)}) collective-permute-start(f32[128,1152]{1,0:T(8,128)S(1)} %get-tuple-element.41), channel_id=1, source_target_pairs={{1,0},{2,1},{3,2},{4,3},{5,4},{6,5},{7,6},{8,7},{9,8},{10,9},{11,1... | collective-permute-start | bytes 1769480 | tf_op jit(solution)/shard_map/return_2/ppermute | solution.py:319
  83.3 0.0 collective-permute-done.22.refs_3_
  83.3 0.0 collective-permute-start.23
  83.3 0.1 collective-permute-done.19.refs_0_
  83.4 1.3 %collective-permute-start.25 = (f32[64,1152]{1,0:T(8,128)S(1)}, f32[64,1152]{1,0:T(8,128)S(1)}, u32[]{:S(2)}, u32[]{:S(2)}) collective-permute-start(f32[64,1152]{1,0:T(8,128)S(1)} %collective-permute-done.19.refs_0_), channel_id=1, source_target_pairs={{0,16},{16,32},{32,48},{48,64},{64,80},{80,96},{96,112},{112,0},{1... | collective-permute-start | bytes 884744 | tf_op jit(solution)/shard_map/piece_1_4/ppermute | solution.py:121
  84.7 0.0 collective-permute-done.20.refs_6_
  84.8 0.0 collective-permute-done.21.refs_1_
  84.8 3.8 %shard_map.49 = (f32[128,1152]{1,0:T(8,128)S(1)}, f32[128,1152]{1,0:T(8,128)S(1)}) custom-call(s32[17]{0:T(128)S(1)} %dynamic-slice_bitcast_fusion.flag.table, f32[64,1152]{1,0:T(8,128)S(1)} %collective-permute-done.19.refs_0_, f32[64,1152]{1,0:T(8,128)S(1)} %collective-permute-done.21.refs_1_, f32[64,1152]{1,0:T(8,128)S(1)} %collective-permute-done.18.refs_2_, ...), custom_call_target="tpu_custom_call" | custom-call | flops 2038431744 | bytes 7667712 | tf_op jit(solution)/shard_map/pallas_call | solution.py:188
  88.6 0.9 collective-permute-start.26
  89.5 2.4 %collective-permute-done.23.refs_0_ = f32[64,1152]{1,0:T(8,128)S(1)} collective-permute-done((f32[64,1152]{1,0:T(8,128)S(1)}, f32[64,1152]{1,0:T(8,128)S(1)}, u32[]{:S(2)}, u32[]{:S(2)}) %collective-permute-start.23) | collective-permute-done | bytes 294944 | tf_op jit(solution)/shard_map/piece_1_3/ppermute | solution.py:121
  91.8 0.0 collective-permute-done.25.refs_1_
  91.8 2.3 %shard_map.50 = (f32[64,1152]{1,0:T(8,128)S(1)}, f32[64,1152]{1,0:T(8,128)S(1)}) custom-call(s32[17]{0:T(128)S(1)} %dynamic-slice_bitcast_fusion.flag.table, f32[64,1152]{1,0:T(8,128)S(1)} %collective-permute-done.23.refs_0_, f32[64,1152]{1,0:T(8,128)S(1)} %collective-permute-done.25.refs_1_, bf16[1152,1152]{1,0:T(8,128)(2,1)S(1)} %get-tuple-element.31.refs_2_.refs_4_, ...), custom_call_target="tpu_custom_call" | custom-call | flops 1019215872 | bytes 6488064 | tf_op jit(solution)/shard_map/pallas_call | solution.py:188
  94.1 2.4 %collective-permute-start.27 = (f32[64,1152]{1,0:T(8,128)S(1)}, f32[64,1152]{1,0:T(8,128)S(1)}, u32[]{:S(2)}, u32[]{:S(2)}) collective-permute-start(f32[64,1152]{1,0:T(8,128)S(1)} %get-tuple-element.48), channel_id=1, source_target_pairs={{1,0},{2,1},{3,2},{4,3},{5,4},{6,5},{7,6},{8,7},{9,8},{10,9},{11,1... | collective-permute-start | bytes 884744 | tf_op jit(solution)/shard_map/return_4/ppermute | solution.py:319
  96.6 3.6 %shard_map.51.held = f32[512,1152]{1,0:T(8,128)} custom-call(s32[17]{0:T(128)S(1)} %dynamic-slice_bitcast_fusion.flag.table, f32[2]{0:T(128)S(1)} %pad_maximum_fusion.factors, f32[512,1152]{1,0:T(8,128)S(1)} %copy-done, f32[64,1152]{1,0:T(8,128)S(1)} %get-tuple-element.33.refs_0_, f32[128,1152]{1,0:T(8,128)S(1)} %get-tuple-element.34.refs_1_, ...), custom_call_target="tpu_custom_call" | custom-call | flops 2875392 | bytes 11501568 | tf_op jit(solution)/shard_map/pallas_call | solution.py:235
  100.2 1.3 %collective-permute-done.27.refs_1_ = f32[64,1152]{1,0:T(8,128)S(1)} collective-permute-done((f32[64,1152]{1,0:T(8,128)S(1)}, f32[64,1152]{1,0:T(8,128)S(1)}, u32[]{:S(2)}, u32[]{:S(2)}) %collective-permute-start.27) | collective-permute-done | bytes 294944 | tf_op jit(solution)/shard_map/return_4/ppermute | solution.py:319
  101.5 2.5 %shard_map.52 = f32[512,1152]{1,0:T(8,128)} custom-call(s32[17]{0:T(128)S(1)} %dynamic-slice_bitcast_fusion.flag.table, f32[2]{0:T(128)S(1)} %pad_maximum_fusion.factors, f32[512,1152]{1,0:T(8,128)} %shard_map.51.held, f32[128,1152]{1,0:T(8,128)S(1)} %collective-permute-done.26.refs_0_, ...), custom_call_target="tpu_custom_call", output_to_operand_aliasing={{}: (2, {})} | custom-call | tf_op jit(solution)/shard_map/pallas_call | solution.py:279
  (8 shorter events, 0.0 us)
Async XLA Ops:
  0.0 3.9 %copy-start = (f32[512,1152]{1,0:T(8,128)S(1)}, f32[512,1152]{1,0:T(8,128)}, u32[]{:S(2)}) copy-start(f32[512,1152]{1,0:T(8,128)} %x.1) | copy-start | bytes 7077892
  2.5 8.2 %collective-permute-start.5 = (f32[128,1152]{1,0:T(8,128)}, f32[128,1152]{1,0:T(8,128)S(1)}, u32[]{:S(2)}, u32[]{:S(2)}) collective-permute-start(f32[128,1152]{1,0:T(8,128)} %get-tuple-element.56), channel_id=1, source_target_pairs={{0,4},{15,3},{17,19},{16,20},{34,38},{33,37},{51,177},{50,54},{68,... | collective-permute-start | bytes 1769480 | tf_op jit(solution)/shard_map/ppermute | solution.py:107
  3.2 8.2 %collective-permute-start.4 = (f32[128,1152]{1,0:T(8,128)}, f32[128,1152]{1,0:T(8,128)S(1)}, u32[]{:S(2)}, u32[]{:S(2)}) collective-permute-start(f32[128,1152]{1,0:T(8,128)} %get-tuple-element.55), channel_id=1, source_target_pairs={{0,128},{15,143},{17,29},{16,146},{34,162},{33,161},{51,63},{50,48... | collective-permute-start | bytes 1769480 | tf_op jit(solution)/shard_map/ppermute | solution.py:107
  4.9 7.2 %collective-permute-start.3 = (f32[64,1152]{1,0:T(8,128)}, f32[64,1152]{1,0:T(8,128)}, u32[]{:S(2)}, u32[]{:S(2)}) collective-permute-start(f32[64,1152]{1,0:T(8,128)} %get-tuple-element.52), channel_id=1, source_target_pairs={{0,208},{15,48},{17,81},{16,65},{34,242},{33,82},{51,115},{50,99},... | collective-permute-start | bytes 884744 | tf_op jit(solution)/shard_map/ppermute | solution.py:108
  6.3 17.2 %collective-permute-start.2 = (f32[64,1152]{1,0:T(8,128)}, f32[64,1152]{1,0:T(8,128)}, u32[]{:S(2)}, u32[]{:S(2)}) collective-permute-start(f32[64,1152]{1,0:T(8,128)} %get-tuple-element.53), channel_id=1, source_target_pairs={{0,64},{15,192},{17,161},{16,1},{34,98},{33,226},{51,195},{50,35},... | collective-permute-start | bytes 884744 | tf_op jit(solution)/shard_map/ppermute | solution.py:108
  7.6 15.9 %collective-permute-start = (f32[64,1152]{1,0:T(8,128)}, f32[64,1152]{1,0:T(8,128)}, u32[]{:S(2)}, u32[]{:S(2)}) collective-permute-start(f32[64,1152]{1,0:T(8,128)} %get-tuple-element.54), channel_id=1, source_target_pairs={{0,32},{15,112},{17,17},{16,209},{34,66},{33,18},{51,51},{50,243},... | collective-permute-start | bytes 884744 | tf_op jit(solution)/shard_map/ppermute | solution.py:108
  10.7 12.8 %collective-permute-start.1 = (f32[64,1152]{1,0:T(8,128)}, f32[64,1152]{1,0:T(8,128)S(1)}, u32[]{:S(2)}, u32[]{:S(2)}) collective-permute-start(f32[64,1152]{1,0:T(8,128)} %get-tuple-element.51), channel_id=1, source_target_pairs={{0,0},{15,224},{17,225},{16,177},{34,34},{33,130},{51,131},{50,211... | collective-permute-start | bytes 884744 | tf_op jit(solution)/shard_map/ppermute | solution.py:108
  11.5 12.0 %collective-permute-start.7 = (f32[64,1152]{1,0:T(8,128)S(1)}, f32[64,1152]{1,0:T(8,128)S(1)}, u32[]{:S(2)}, u32[]{:S(2)}) collective-permute-start(f32[64,1152]{1,0:T(8,128)S(1)} %get-tuple-element.58), channel_id=1, source_target_pairs={{128,144},{4,240},{143,160},{3,16},{29,129},{19,49},{146,241},{20,... | collective-permute-start | bytes 884744 | tf_op jit(solution)/shard_map/ppermute | solution.py:110
  12.2 11.3 %collective-permute-start.6 = (f32[64,1152]{1,0:T(8,128)S(1)}, f32[64,1152]{1,0:T(8,128)S(1)}, u32[]{:S(2)}, u32[]{:S(2)}) collective-permute-start(f32[64,1152]{1,0:T(8,128)S(1)} %get-tuple-element.57), channel_id=1, source_target_pairs={{128,96},{4,176},{143,80},{3,128},{29,193},{19,113},{146,33},{20,9... | collective-permute-start | bytes 884744 | tf_op jit(solution)/shard_map/ppermute | solution.py:110
  24.8 19.5 %collective-permute-start.8 = (f32[64,1152]{1,0:T(8,128)S(1)}, f32[64,1152]{1,0:T(8,128)S(1)}, u32[]{:S(2)}, u32[]{:S(2)}) collective-permute-start(f32[64,1152]{1,0:T(8,128)S(1)} %add_add_fusion.refs_0_), channel_id=1, source_target_pairs={{0,112},{16,0},{32,16},{48,32},{64,48},{80,64},{96,80},{112,96},{1... | collective-permute-start | bytes 884744 | tf_op jit(solution)/shard_map/piece_0_1/ppermute | solution.py:121
  40.1 8.0 %collective-permute-start.10 = (f32[64,1152]{1,0:T(8,128)S(1)}, f32[64,1152]{1,0:T(8,128)S(1)}, u32[]{:S(2)}, u32[]{:S(2)}) collective-permute-start(f32[64,1152]{1,0:T(8,128)S(1)} %add_add_fusion.refs_0_), channel_id=1, source_target_pairs={{0,16},{16,32},{32,48},{48,64},{64,80},{80,96},{96,112},{112,0},{1... | collective-permute-start | bytes 884744 | tf_op jit(solution)/shard_map/piece_0_-1/ppermute | solution.py:121
  40.1 13.7 %collective-permute-start.12 = (f32[64,1152]{1,0:T(8,128)S(1)}, f32[64,1152]{1,0:T(8,128)S(1)}, u32[]{:S(2)}, u32[]{:S(2)}) collective-permute-start(f32[64,1152]{1,0:T(8,128)S(1)} %add_add_fusion.refs_0_), channel_id=1, source_target_pairs={{0,128},{16,144},{32,160},{48,176},{64,192},{80,208},{96,224},{112... | collective-permute-start | bytes 884744 | tf_op jit(solution)/shard_map/piece_1_0/ppermute | solution.py:121
  44.3 10.3 %collective-permute-start.9 = (f32[64,1152]{1,0:T(8,128)S(1)}, f32[64,1152]{1,0:T(8,128)S(1)}, u32[]{:S(2)}, u32[]{:S(2)}) collective-permute-start(f32[64,1152]{1,0:T(8,128)S(1)} %collective-permute-done.8.refs_1_), channel_id=1, source_target_pairs={{0,112},{16,0},{32,16},{48,32},{64,48},{80,64},{96,80},{112,96},{1... | collective-permute-start | bytes 884744 | tf_op jit(solution)/shard_map/piece_0_2/ppermute | solution.py:121
  48.1 11.0 %collective-permute-start.11 = (f32[64,1152]{1,0:T(8,128)S(1)}, f32[64,1152]{1,0:T(8,128)S(1)}, u32[]{:S(2)}, u32[]{:S(2)}) collective-permute-start(f32[64,1152]{1,0:T(8,128)S(1)} %collective-permute-done.10.refs_2_), channel_id=1, source_target_pairs={{0,16},{16,32},{32,48},{48,64},{64,80},{80,96},{96,112},{112,0},{1... | collective-permute-start | bytes 884744 | tf_op jit(solution)/shard_map/piece_0_-2/ppermute | solution.py:121
  48.5 10.6 %collective-permute-start.15 = (f32[64,1152]{1,0:T(8,128)S(1)}, f32[64,1152]{1,0:T(8,128)S(1)}, u32[]{:S(2)}, u32[]{:S(2)}) collective-permute-start(f32[64,1152]{1,0:T(8,128)S(1)} %collective-permute-done.10.refs_2_), channel_id=1, source_target_pairs={{0,128},{16,144},{32,160},{48,176},{64,192},{80,208},{96,224},{112... | collective-permute-start | bytes 884744 | tf_op jit(solution)/shard_map/piece_1_-1/ppermute | solution.py:121
  48.5 16.3 %collective-permute-start.13 = (f32[64,1152]{1,0:T(8,128)S(1)}, f32[64,1152]{1,0:T(8,128)S(1)}, u32[]{:S(2)}, u32[]{:S(2)}) collective-permute-start(f32[64,1152]{1,0:T(8,128)S(1)} %collective-permute-done.8.refs_1_), channel_id=1, source_target_pairs={{0,128},{16,144},{32,160},{48,176},{64,192},{80,208},{96,224},{112... | collective-permute-start | bytes 884744 | tf_op jit(solution)/shard_map/piece_1_1/ppermute | solution.py:121
  53.8 13.4 %collective-permute-start.14 = (f32[64,1152]{1,0:T(8,128)S(1)}, f32[64,1152]{1,0:T(8,128)S(1)}, u32[]{:S(2)}, u32[]{:S(2)}) collective-permute-start(f32[64,1152]{1,0:T(8,128)S(1)} %get-tuple-element.35), channel_id=1, source_target_pairs={{1,0},{2,1},{3,2},{4,3},{5,4},{6,5},{7,6},{8,7},{9,8},{10,9},{11,1... | collective-permute-start | bytes 884744 | tf_op jit(solution)/shard_map/return_0/ppermute | solution.py:319
  54.6 20.2 %collective-permute-start.16 = (f32[64,1152]{1,0:T(8,128)S(1)}, f32[64,1152]{1,0:T(8,128)S(1)}, u32[]{:S(2)}, u32[]{:S(2)}) collective-permute-start(f32[64,1152]{1,0:T(8,128)S(1)} %collective-permute-done.9.refs_0_), channel_id=1, source_target_pairs={{0,112},{16,0},{32,16},{48,32},{64,48},{80,64},{96,80},{112,96},{1... | collective-permute-start | bytes 884744 | tf_op jit(solution)/shard_map/piece_0_3/ppermute | solution.py:121
  59.1 18.4 %collective-permute-start.17 = (f32[64,1152]{1,0:T(8,128)S(1)}, f32[64,1152]{1,0:T(8,128)S(1)}, u32[]{:S(2)}, u32[]{:S(2)}) collective-permute-start(f32[64,1152]{1,0:T(8,128)S(1)} %collective-permute-done.11.refs_1_), channel_id=1, source_target_pairs={{0,16},{16,32},{32,48},{48,64},{64,80},{80,96},{96,112},{112,0},{1... | collective-permute-start | bytes 884744 | tf_op jit(solution)/shard_map/piece_0_-3/ppermute | solution.py:121
  59.1 15.8 %collective-permute-start.18 = (f32[64,1152]{1,0:T(8,128)S(1)}, f32[64,1152]{1,0:T(8,128)S(1)}, u32[]{:S(2)}, u32[]{:S(2)}) collective-permute-start(f32[64,1152]{1,0:T(8,128)S(1)} %collective-permute-done.15.refs_1_), channel_id=1, source_target_pairs={{0,16},{16,32},{32,48},{48,64},{64,80},{80,96},{96,112},{112,0},{1... | collective-permute-start | bytes 884744 | tf_op jit(solution)/shard_map/piece_1_-2/ppermute | solution.py:121
  64.8 19.9 %collective-permute-start.20 = (f32[128,1152]{1,0:T(8,128)S(1)}, f32[128,1152]{1,0:T(8,128)S(1)}, u32[]{:S(2)}, u32[]{:S(2)}) collective-permute-start(f32[128,1152]{1,0:T(8,128)S(1)} %get-tuple-element.38), channel_id=1, source_target_pairs={{1,0},{2,1},{3,2},{4,3},{5,4},{6,5},{7,6},{8,7},{9,8},{10,9},{11,1... | collective-permute-start | bytes 1769480 | tf_op jit(solution)/shard_map/return_1/ppermute | solution.py:319
  67.3 16.0 %collective-permute-start.22 = (f32[64,1152]{1,0:T(8,128)S(1)}, f32[64,1152]{1,0:T(8,128)S(1)}, u32[]{:S(2)}, u32[]{:S(2)}) collective-permute-start(f32[64,1152]{1,0:T(8,128)S(1)} %collective-permute-done.13.refs_0_), channel_id=1, source_target_pairs={{0,112},{16,0},{32,16},{48,32},{64,48},{80,64},{96,80},{112,96},{1... | collective-permute-start | bytes 884744 | tf_op jit(solution)/shard_map/piece_1_2/ppermute | solution.py:121
  74.9 8.5 %collective-permute-start.19 = (f32[64,1152]{1,0:T(8,128)S(1)}, f32[64,1152]{1,0:T(8,128)S(1)}, u32[]{:S(2)}, u32[]{:S(2)}) collective-permute-start(f32[64,1152]{1,0:T(8,128)S(1)} %collective-permute-done.18.refs_2_), channel_id=1, source_target_pairs={{0,16},{16,32},{32,48},{48,64},{64,80},{80,96},{96,112},{112,0},{1... | collective-permute-start | bytes 884744 | tf_op jit(solution)/shard_map/piece_1_-3/ppermute | solution.py:121
  74.9 9.9 %collective-permute-start.21 = (f32[64,1152]{1,0:T(8,128)S(1)}, f32[64,1152]{1,0:T(8,128)S(1)}, u32[]{:S(2)}, u32[]{:S(2)}) collective-permute-start(f32[64,1152]{1,0:T(8,128)S(1)} %collective-permute-done.16.refs_2_), channel_id=1, source_target_pairs={{0,112},{16,0},{32,16},{48,32},{64,48},{80,64},{96,80},{112,96},{1... | collective-permute-start | bytes 884744 | tf_op jit(solution)/shard_map/piece_0_4/ppermute | solution.py:121
  81.4 10.4 %collective-permute-start.24 = (f32[128,1152]{1,0:T(8,128)S(1)}, f32[128,1152]{1,0:T(8,128)S(1)}, u32[]{:S(2)}, u32[]{:S(2)}) collective-permute-start(f32[128,1152]{1,0:T(8,128)S(1)} %get-tuple-element.41), channel_id=1, source_target_pairs={{1,0},{2,1},{3,2},{4,3},{5,4},{6,5},{7,6},{8,7},{9,8},{10,9},{11,1... | collective-permute-start | bytes 1769480 | tf_op jit(solution)/shard_map/return_2/ppermute | solution.py:319
  83.3 8.6 %collective-permute-start.23 = (f32[64,1152]{1,0:T(8,128)S(1)}, f32[64,1152]{1,0:T(8,128)S(1)}, u32[]{:S(2)}, u32[]{:S(2)}) collective-permute-start(f32[64,1152]{1,0:T(8,128)S(1)} %collective-permute-done.22.refs_3_), channel_id=1, source_target_pairs={{0,112},{16,0},{32,16},{48,32},{64,48},{80,64},{96,80},{112,96},{1... | collective-permute-start | bytes 884744 | tf_op jit(solution)/shard_map/piece_1_3/ppermute | solution.py:121
  83.4 8.4 %collective-permute-start.25 = (f32[64,1152]{1,0:T(8,128)S(1)}, f32[64,1152]{1,0:T(8,128)S(1)}, u32[]{:S(2)}, u32[]{:S(2)}) collective-permute-start(f32[64,1152]{1,0:T(8,128)S(1)} %collective-permute-done.19.refs_0_), channel_id=1, source_target_pairs={{0,16},{16,32},{32,48},{48,64},{64,80},{80,96},{96,112},{112,0},{1... | collective-permute-start | bytes 884744 | tf_op jit(solution)/shard_map/piece_1_4/ppermute | solution.py:121
  88.6 12.9 %collective-permute-start.26 = (f32[128,1152]{1,0:T(8,128)S(1)}, f32[128,1152]{1,0:T(8,128)S(1)}, u32[]{:S(2)}, u32[]{:S(2)}) collective-permute-start(f32[128,1152]{1,0:T(8,128)S(1)} %get-tuple-element.47), channel_id=1, source_target_pairs={{1,0},{2,1},{3,2},{4,3},{5,4},{6,5},{7,6},{8,7},{9,8},{10,9},{11,1... | collective-permute-start | bytes 1769480 | tf_op jit(solution)/shard_map/return_3/ppermute | solution.py:319
  94.1 7.3 %collective-permute-start.27 = (f32[64,1152]{1,0:T(8,128)S(1)}, f32[64,1152]{1,0:T(8,128)S(1)}, u32[]{:S(2)}, u32[]{:S(2)}) collective-permute-start(f32[64,1152]{1,0:T(8,128)S(1)} %get-tuple-element.48), channel_id=1, source_target_pairs={{1,0},{2,1},{3,2},{4,3},{5,4},{6,5},{7,6},{8,7},{9,8},{10,9},{11,1... | collective-permute-start | bytes 884744 | tf_op jit(solution)/shard_map/return_4/ppermute | solution.py:319

commit v3 on v2

--- a/solution.py
+++ b/solution.py
@@ -13,10 +13,10 @@
 OTHER = ((0, 1), (0, -1), (1, 0), (0, 3), (0, -3), (1, -2), (1, 2), (1, 4))
 GROUPS = ((0, 1), (1, 3), (3, 5), (5, 7), (7, 8))
 PLAN = {
-    (0, 0): (((2, 0), (0, 1)), (((0, 2), (0, 0), (0, 4), (1, 5)), ((0, 6), (1, 1)), ((1, 3), (1, 7)))),
-    (0, 1): (((0, 3), (1, 0)), (((0, 0), (1, 5), (1, 1), (0, 4)), ((1, 3), (1, 7)), ((0, 6), (0, 2)))),
-    (1, 0): (((2, 0), (0, 1)), (((0, 7), (1, 6), (1, 4), (0, 3)), ((0, 5), (1, 2)), ((1, 0), (0, 1)))),
-    (1, 1): (((3, 0), (0, 1)), (((1, 4), (1, 2), (0, 7), (0, 3)), ((0, 1), (1, 6)), ((0, 5), (1, 0)))),
+    (0, 0): (((2, 0), (0, 1)), (((0, 0), (1, 5), (0, 4), (0, 2)), ((1, 1), (0, 6)), ((1, 3), (1, 7)))),
+    (0, 1): (((0, 3), (1, 0)), (((0, 0), (0, 4), (1, 1), (1, 5)), ((1, 7), (1, 3)), ((0, 6), (0, 2)))),
+    (1, 0): (((2, 0), (0, 1)), (((0, 7), (0, 3), (1, 4), (1, 6)), ((1, 2), (0, 5)), ((1, 0), (0, 1)))),
+    (1, 1): (((3, 0), (0, 1)), (((0, 7), (1, 2), (1, 4), (0, 3)), ((0, 1), (1, 6)), ((0, 5), (1, 0)))),
 }
 
 
@@ -66,25 +66,75 @@
         return (label[0] ^ kind, (label[1] + d) % self.ring)
 
     def tables(self):
-        out = np.zeros((self.n, self.n, 17), np.int32)
+        out = np.zeros((self.n, self.n, 18), np.int32)
         for row in range(self.n):
             for col in range(self.n):
                 mine = self.label(row, col)
                 out[row, col, 0] = sum(mine) % 2
                 kept = OTHER if sum(mine) % 2 else SAME
+                at = slot_of(sum(mine) % 2, col, mine)
+                out[row, col, 17] = at if at < 4 else 4 + at % 2
                 theirs = self.label(row, (col + 1) % self.n)
                 sent = SAME if sum(theirs) % 2 else OTHER
                 for i in range(8):
                     out[row, col, 1 + i] = slot_of(0, col, self.near(mine, *kept[i]))
                     out[row, col, 9 + i] = slot_of(1, col + 1, self.near(theirs, *sent[i]))
-        return out.reshape(self.n * self.n, 17)
+        return out.reshape(self.n * self.n, 18)
 
 
 def slot_of(block, c, label):
     return [h for holders in PLAN[block, c % 2][1] for h in holders].index(label)
 
 
-def spread(x, grid):
+def cut_body(starts, x, *refs):
+    outs, leave = refs[:-1], refs[-1]
+    copies = [
+        pltpu.make_async_copy(x.at[pl.ds(at, out.shape[0])], out, leave.at[i])
+        for i, (at, out) in enumerate(zip(starts, outs))
+    ]
+    for copy in copies:
+        copy.start()
+    for copy in copies:
+        copy.wait()
+
+
+def cut(x, eighths):
+    size, free = x.shape[0] // 8, pl.BlockSpec(memory_space=pl.ANY)
+    return pl.pallas_call(
+        functools.partial(cut_body, [size * sum(eighths[:i]) for i in range(len(eighths))]),
+        out_shape=tuple(jax.ShapeDtypeStruct((size * n, x.shape[1]), x.dtype) for n in eighths),
+        in_specs=[pl.BlockSpec(memory_space=pltpu.HBM)],
+        out_specs=(free,) * len(eighths),
+        scratch_shapes=[pltpu.SemaphoreType.DMA((len(eighths),))],
+        compiler_params=pltpu.CompilerParams(vmem_limit_bytes=1 << 20),
+        cost_estimate=pl.CostEstimate(flops=0, bytes_accessed=8 * x.size, transcendentals=0),
+    )(x)
+
+
+def pick_body(table, *refs):
+    *parts, out, arrive = refs
+    for i, part in enumerate(parts):
+
+        @pl.when(table[17] == i)
+        def _():
+            copy = pltpu.make_async_copy(part, out, arrive)
+            copy.start()
+            copy.wait()
+
+
+def pick(table, parts):
+    free = pl.BlockSpec(memory_space=pl.ANY)
+    return pl.pallas_call(
+        pick_body,
+        out_shape=jax.ShapeDtypeStruct(parts[0].shape, parts[0].dtype),
+        in_specs=[pl.BlockSpec(memory_space=pltpu.SMEM)] + [free] * len(parts),
+        out_specs=free,
+        scratch_shapes=[pltpu.SemaphoreType.DMA],
+        compiler_params=pltpu.CompilerParams(vmem_limit_bytes=1 << 20),
+    )(table, *parts)
+
+
+def spread(x, table, grid):
     size = x.shape[0] // 8
     groups = [(c, b) for c in range(grid.n) for b in range(2)]
 
@@ -104,11 +154,12 @@
             for s in who
         ]
 
-    held = [lax.ppermute(x[4 * size : 6 * size], BOTH, hop(1)), lax.ppermute(x[6 * size :], BOTH, hop(2))]
-    got = [lax.ppermute(x[size * j : size * (j + 1)], BOTH, deal((0,), j)) for j in range(4)]
+    *eighths, third, fourth = cut(x, (1, 1, 1, 1, 2, 2))
+    held = [lax.ppermute(third, BOTH, hop(1)), lax.ppermute(fourth, BOTH, hop(2))]
+    got = [lax.ppermute(eighths[j], BOTH, deal((0,), j)) for j in range(4)]
     both = [held[0][size * j : size * (j + 1)] + held[1][size * j : size * (j + 1)] for j in range(2)]
     got += [lax.ppermute(both[j], BOTH, deal((1, 2), j)) for j in range(2)]
-    return functools.reduce(jnp.add, got), both
+    return pick(table, got), both
 
 
 def after(value, *others):
@@ -207,10 +258,10 @@
 
 
 def finish_body(n, table, factors, x, *refs):
-    parts, (out, f, g, arrive, leave) = refs[:-5], refs[-5:]
+    parts, (out, g, arrive) = refs[:-3], refs[-3:]
     keep, lean = factors[0], factors[1]
     size = x.shape[0] // 8
-    loads, lo = [pltpu.make_async_copy(x, f, arrive.at[0])], 0
+    loads, lo = [pltpu.make_async_copy(x, out, arrive.at[0])], 0
     for ref in parts:
         rows = ref.shape[0]
         loads.append(pltpu.make_async_copy(ref, g.at[pl.ds(lo, rows)], arrive.at[len(loads)]))
@@ -221,11 +272,8 @@
         load.wait()
     for i in range(n):
         at = pl.ds(pl.multiple_of(table[1 + i] * size, size), size)
-        held = keep * f[at, :] if i < 8 else f[at, :]
-        f[at, :] = held + lean * g[i * size : (i + 1) * size, :]
-    store = pltpu.make_async_copy(f, out, leave.at[0])
-    store.start()
-    store.wait()
+        held = keep * out[at, :] if i < 8 else out[at, :]
+        out[at, :] = held + lean * g[i * size : (i + 1) * size, :]
 
 
 def finish(table, factors, x, parts):
@@ -236,12 +284,10 @@
         functools.partial(finish_body, rows * 8 // x.shape[0]),
         out_shape=jax.ShapeDtypeStruct(x.shape, jnp.float32),
         in_specs=[smem, smem] + [free] * (1 + len(parts)),
-        out_specs=free,
+        out_specs=pl.BlockSpec(memory_space=pltpu.VMEM),
         scratch_shapes=[
-            pltpu.VMEM(x.shape, jnp.float32),
             pltpu.VMEM((rows, x.shape[1]), jnp.float32),
             pltpu.SemaphoreType.DMA((1 + len(parts),)),
-            pltpu.SemaphoreType.DMA((1,)),
         ],
         compiler_params=pltpu.CompilerParams(vmem_limit_bytes=14 << 20),
         cost_estimate=pl.CostEstimate(
@@ -251,21 +297,19 @@
 
 
 def last_body(first, table, factors, held, *refs):
-    parts, (out, f, arrive, leave) = refs[:-4], refs[-4:]
+    parts, (out, f, leave) = refs[:-3], refs[-3:]
     size = held.shape[0] // 8
-    n = f.shape[0] // size
-    at = [pl.ds(pl.multiple_of(table[9 + first + i] * size, size), size) for i in range(n)]
-    mine = [pl.ds(i * size, size) for i in range(n)]
-    loads = [pltpu.make_async_copy(held.at[at[i]], f.at[mine[i]], arrive.at[i]) for i in range(n)]
-    stores = [pltpu.make_async_copy(f.at[mine[i]], out.at[at[i]], leave.at[i]) for i in range(n)]
-    for load in loads:
-        load.start()
+    at = [pl.ds(pl.multiple_of(table[9 + i] * size, size), size) for i in range(8)]
+    mine = [pl.ds(i * size, size) for i in range(8 - first)]
+    stores = [pltpu.make_async_copy(held.at[at[i]], out.at[at[i]], leave.at[i]) for i in range(first)]
+    for store in stores:
+        store.start()
     i = 0
     for part in parts:
         for lo in range(0, part.shape[0], size):
-            loads[i].wait()
-            f[mine[i], :] = f[mine[i], :] + factors[1] * part[lo : lo + size, :]
-            stores[i].start()
+            f[mine[i], :] = held[at[first + i], :] + factors[1] * part[lo : lo + size, :]
+            stores.append(pltpu.make_async_copy(f.at[mine[i]], out.at[at[first + i]], leave.at[first + i]))
+            stores[-1].start()
             i += 1
     for store in stores:
         store.wait()
@@ -275,17 +319,14 @@
     free = pl.BlockSpec(memory_space=pl.ANY)
     smem = pl.BlockSpec(memory_space=pltpu.SMEM)
     vmem = pl.BlockSpec(memory_space=pltpu.VMEM)
-    n = 8 - first
     return pl.pallas_call(
         functools.partial(last_body, first),
         out_shape=jax.ShapeDtypeStruct(held.shape, jnp.float32),
-        in_specs=[smem, smem, free] + [vmem] * len(parts),
+        in_specs=[smem, smem, vmem] + [vmem] * len(parts),
         out_specs=free,
-        input_output_aliases={2: 0},
         scratch_shapes=[
-            pltpu.VMEM((held.shape[0] // 8 * n, held.shape[1]), jnp.float32),
-            pltpu.SemaphoreType.DMA((n,)),
-            pltpu.SemaphoreType.DMA((n,)),
+            pltpu.VMEM((held.shape[0] // 8 * (8 - first), held.shape[1]), jnp.float32),
+            pltpu.SemaphoreType.DMA((8,)),
         ],
         compiler_params=pltpu.CompilerParams(vmem_limit_bytes=6 << 20),
     )(table, factors, held, *parts)
@@ -295,7 +336,7 @@
     here = lax.axis_index("row") * grid.n + lax.axis_index("col")
     table = lax.dynamic_index_in_dim(jnp.asarray(grid.tables()), here, 0, keepdims=False)
     factors = jnp.stack(coefficients(lower))
-    piece, relayed = spread(iterate, grid)
+    piece, relayed = spread(iterate, table, grid)
     inverse = after(inverse, *relayed)
     high = inverse.astype(jnp.bfloat16)
     low = (inverse - lax.reduce_precision(inverse, 8, 7)).astype(jnp.bfloat16)

time: 105 us -> 103 us (0.981)
  the two profiles are of different devices: /device:TPU:1 before, /device:TPU:127 now
where the time goes in v3:
time: 103 us; the launch traced here: 102 us
  starting transfers between devices  53.7 us (52%)
  Pallas kernels  21.5 us (21%)
  waiting for transfers between devices  16.9 us (16%)
  other arithmetic  6.37 us (6%)
  local copies, waits for them, and re-layouts  2.37 us (2%)
  between operations  1.31 us (1%)
    ppermute x15, starting transfers between devices, move(): return lax.ppermute(after(v, *others) if others else v, 'row', route)  31 us
    pallas_call x5, Pallas kernels, product(): pl.pallas_call(functools.partial(product_body, n), out_shape=(shape, shap...  16.2 us
    ppermute x5, starting transfers between devices, send(): sent.append(lax.ppermute(go, 'col', back))  15.1 us
    ppermute x15, waiting for transfers between devices, move(): return lax.ppermute(after(v, *others) if others else v, 'row', route)  8.69 us
    ppermute x5, waiting for transfers between devices, send(): sent.append(lax.ppermute(go, 'col', back))  5.66 us
    convert_element_type x1, other arithmetic, shards(): low = (inverse - lax.reduce_precision(inverse, 8, 7)).astype(jnp.bfloat16)  5.01 us
    ppermute x4, starting transfers between devices, spread(): got = [lax.ppermute(eighths[j], BOTH, deal((0,), j)) for j in range(4)]  3.31 us
    ppermute x4, waiting for transfers between devices, spread(): got = [lax.ppermute(eighths[j], BOTH, deal((0,), j)) for j in range(4)]  2.58 us
  transfers between devices with their start and end apart: 28, of which 5 were waited for; matrix products, arithmetic and copies ran while one was open for 7% of the time, Pallas kernels for 18%

profile of v3, /device:TPU:127, one launch (start us, length us, event | category | flops | bytes accessed | tf_op | source)
XLA Modules:
  0.0 102.3 jit_solution(2087673228837730130)
XLA Ops:
  0.0 1.7 %copy-done = f32[512,1152]{1,0:T(8,128)S(1)} copy-done((f32[512,1152]{1,0:T(8,128)S(1)}, f32[512,1152]{1,0:T(8,128)}, u32[]{:S(2)}) %copy-start) | copy-done | bytes 2359320
  1.7 0.5 shard_map.46
  2.2 1.5 %collective-permute-start.5 = (f32[128,1152]{1,0:T(8,128)S(1)}, f32[128,1152]{1,0:T(8,128)}, u32[]{:S(2)}, u32[]{:S(2)}) collective-permute-start(f32[128,1152]{1,0:T(8,128)S(1)} %get-tuple-element.38), channel_id=1, source_target_pairs={{0,4},{15,3},{17,19},{16,20},{34,38},{33,37},{51,177},{50,54},{68,... | collective-permute-start | bytes 1769480 | tf_op jit(solution)/shard_map/ppermute | solution.py:158
  3.7 1.5 %collective-permute-start.4 = (f32[128,1152]{1,0:T(8,128)S(1)}, f32[128,1152]{1,0:T(8,128)}, u32[]{:S(2)}, u32[]{:S(2)}) collective-permute-start(f32[128,1152]{1,0:T(8,128)S(1)} %get-tuple-element.37), channel_id=1, source_target_pairs={{0,128},{15,143},{17,29},{16,146},{34,162},{33,161},{51,63},{50,48... | collective-permute-start | bytes 1769480 | tf_op jit(solution)/shard_map/ppermute | solution.py:158
  5.2 0.7 collective-permute-start
  5.9 1.3 %collective-permute-start.1 = (f32[64,1152]{1,0:T(8,128)S(1)}, f32[64,1152]{1,0:T(8,128)S(1)}, u32[]{:S(2)}, u32[]{:S(2)}) collective-permute-start(f32[64,1152]{1,0:T(8,128)S(1)} %get-tuple-element.34), channel_id=1, source_target_pairs={{0,208},{15,48},{17,81},{16,177},{34,242},{33,82},{51,115},{50,211... | collective-permute-start | bytes 884744 | tf_op jit(solution)/shard_map/ppermute | solution.py:159
  7.2 0.7 collective-permute-start.2
  8.8 0.7 dynamic-slice_bitcast_fusion.table.flag
  9.5 0.1 pad_maximum_fusion.factors
  9.6 0.0 collective-permute-done.5
  9.6 0.7 collective-permute-start.3
  10.2 0.0 collective-permute-done.4
  10.3 1.3 %slice_add_fusion = (f32[64,1152]{1,0:T(8,128)S(1)}, f32[64,1152]{1,0:T(8,128)S(1)}) fusion(f32[128,1152]{1,0:T(8,128)} %collective-permute-done.5, f32[128,1152]{1,0:T(8,128)} %collective-permute-done.4), kind=kLoop, calls=%fused_computation.2 | loop fusion | flops 147456 | bytes 1769472 | tf_op jit(solution)/shard_map/add | solution.py:160
  11.6 0.7 collective-permute-start.6
  12.2 0.0 collective-permute-done.refs_0_
  12.3 0.7 collective-permute-start.7
  12.9 5.0 %fusion = (bf16[1152,1152]{1,0:T(8,128)(2,1)S(1)}, bf16[1152,1152]{1,0:T(8,128)(2,1)S(1)}) fusion(f32[1152,1152]{1,0:T(8,128)} %param.5), kind=kLoop, calls=%fused_computation.1 | loop fusion | flops 5308416 | bytes 10616832 | tf_op jit(solution)/shard_map/convert_element_type | solution.py:342
  17.9 2.6 %collective-permute-done.1.refs_1_ = f32[64,1152]{1,0:T(8,128)S(1)} collective-permute-done((f32[64,1152]{1,0:T(8,128)S(1)}, f32[64,1152]{1,0:T(8,128)S(1)}, u32[]{:S(2)}, u32[]{:S(2)}) %collective-permute-start.1) | collective-permute-done | bytes 294944 | tf_op jit(solution)/shard_map/ppermute | solution.py:159
  20.5 0.0 collective-permute-done.2.refs_2_
  20.5 0.0 collective-permute-done.3.refs_3_
  20.5 0.0 collective-permute-done.6.refs_4_
  20.5 0.0 collective-permute-done.7.refs_5_
  20.5 0.7 shard_map.47.refs_0_
  21.2 11.5 %collective-permute-start.8 = (f32[64,1152]{1,0:T(8,128)S(1)}, f32[64,1152]{1,0:T(8,128)S(1)}, u32[]{:S(2)}, u32[]{:S(2)}) collective-permute-start(f32[64,1152]{1,0:T(8,128)S(1)} %shard_map.47.refs_0_), channel_id=1, source_target_pairs={{0,112},{16,0},{32,16},{48,32},{64,48},{80,64},{96,80},{112,96},{1... | collective-permute-start | bytes 884744 | tf_op jit(solution)/shard_map/piece_0_1/ppermute | solution.py:172
  32.7 0.0 collective-permute-start.10
  32.7 2.3 %collective-permute-start.12 = (f32[64,1152]{1,0:T(8,128)S(1)}, f32[64,1152]{1,0:T(8,128)S(1)}, u32[]{:S(2)}, u32[]{:S(2)}) collective-permute-start(f32[64,1152]{1,0:T(8,128)S(1)} %shard_map.47.refs_0_), channel_id=1, source_target_pairs={{0,128},{16,144},{32,160},{48,176},{64,192},{80,208},{96,224},{112... | collective-permute-start | bytes 884744 | tf_op jit(solution)/shard_map/piece_1_0/ppermute | solution.py:172
  35.0 1.8 %collective-permute-done.8.refs_1_ = f32[64,1152]{1,0:T(8,128)S(1)} collective-permute-done((f32[64,1152]{1,0:T(8,128)S(1)}, f32[64,1152]{1,0:T(8,128)S(1)}, u32[]{:S(2)}, u32[]{:S(2)}) %collective-permute-start.8) | collective-permute-done | bytes 294944 | tf_op jit(solution)/shard_map/piece_0_1/ppermute | solution.py:172
  36.8 3.1 %collective-permute-start.9 = (f32[64,1152]{1,0:T(8,128)S(1)}, f32[64,1152]{1,0:T(8,128)S(1)}, u32[]{:S(2)}, u32[]{:S(2)}) collective-permute-start(f32[64,1152]{1,0:T(8,128)S(1)} %collective-permute-done.8.refs_1_), channel_id=1, source_target_pairs={{0,112},{16,0},{32,16},{48,32},{64,48},{80,64},{96,80},{112,96},{1... | collective-permute-start | bytes 884744 | tf_op jit(solution)/shard_map/piece_0_2/ppermute | solution.py:172
  39.9 0.0 collective-permute-done.10.refs_2_
  39.9 0.0 collective-permute-start.11
  39.9 2.7 %collective-permute-start.15 = (f32[64,1152]{1,0:T(8,128)S(1)}, f32[64,1152]{1,0:T(8,128)S(1)}, u32[]{:S(2)}, u32[]{:S(2)}) collective-permute-start(f32[64,1152]{1,0:T(8,128)S(1)} %collective-permute-done.10.refs_2_), channel_id=1, source_target_pairs={{0,128},{16,144},{32,160},{48,176},{64,192},{80,208},{96,224},{112... | collective-permute-start | bytes 884744 | tf_op jit(solution)/shard_map/piece_1_-1/ppermute | solution.py:172
  42.6 0.3 collective-permute-start.13
  42.9 2.3 %shard_map.48 = (f32[64,1152]{1,0:T(8,128)S(1)}, f32[64,1152]{1,0:T(8,128)S(1)}) custom-call(s32[18]{0:T(128)S(1)} %dynamic-slice_bitcast_fusion.table.flag, f32[64,1152]{1,0:T(8,128)S(1)} %shard_map.47.refs_0_, f32[64,1152]{1,0:T(8,128)S(1)} %collective-permute-done.8.refs_1_, bf16[1152,1152]{1,0:T(8,128)(2,1)S(1)} %get-tuple-element.43.refs_2_.refs_4_, ...), custom_call_target="tpu_custom_call" | custom-call | flops 1019215872 | bytes 6488064 | tf_op jit(solution)/shard_map/pallas_call | solution.py:239
  45.2 0.0 collective-permute-done.12.refs_3_
  45.2 9.2 %collective-permute-start.14 = (f32[64,1152]{1,0:T(8,128)S(1)}, f32[64,1152]{1,0:T(8,128)S(1)}, u32[]{:S(2)}, u32[]{:S(2)}) collective-permute-start(f32[64,1152]{1,0:T(8,128)S(1)} %get-tuple-element.47), channel_id=1, source_target_pairs={{1,0},{2,1},{3,2},{4,3},{5,4},{6,5},{7,6},{8,7},{9,8},{10,9},{11,1... | collective-permute-start | bytes 884744 | tf_op jit(solution)/shard_map/return_0/ppermute | solution.py:360
  54.4 0.0 collective-permute-done.9.refs_0_
  54.4 0.0 collective-permute-start.16
  54.4 2.7 %collective-permute-start.17 = (f32[64,1152]{1,0:T(8,128)S(1)}, f32[64,1152]{1,0:T(8,128)S(1)}, u32[]{:S(2)}, u32[]{:S(2)}) collective-permute-start(f32[64,1152]{1,0:T(8,128)S(1)} %collective-permute-done.11.refs_1_), channel_id=1, source_target_pairs={{0,16},{16,32},{32,48},{48,64},{64,80},{80,96},{96,112},{112,0},{1... | collective-permute-start | bytes 884744 | tf_op jit(solution)/shard_map/piece_0_-3/ppermute | solution.py:172
  57.1 0.0 collective-permute-done.15.refs_1_
  57.1 0.3 collective-permute-start.18
  57.4 3.8 %shard_map.49 = (f32[128,1152]{1,0:T(8,128)S(1)}, f32[128,1152]{1,0:T(8,128)S(1)}) custom-call(s32[18]{0:T(128)S(1)} %dynamic-slice_bitcast_fusion.table.flag, f32[64,1152]{1,0:T(8,128)S(1)} %collective-permute-done.9.refs_0_, f32[64,1152]{1,0:T(8,128)S(1)} %collective-permute-done.11.refs_1_, f32[64,1152]{1,0:T(8,128)S(1)} %collective-permute-done.10.refs_2_, ...), custom_call_target="tpu_custom_call" | custom-call | flops 2038431744 | bytes 7667712 | tf_op jit(solution)/shard_map/pallas_call | solution.py:239
  61.3 0.7 collective-permute-start.20
  62.0 0.0 collective-permute-done.14.refs_5_
  62.0 1.5 %collective-permute-start.22 = (f32[64,1152]{1,0:T(8,128)S(1)}, f32[64,1152]{1,0:T(8,128)S(1)}, u32[]{:S(2)}, u32[]{:S(2)}) collective-permute-start(f32[64,1152]{1,0:T(8,128)S(1)} %collective-permute-done.13.refs_0_), channel_id=1, source_target_pairs={{0,112},{16,0},{32,16},{48,32},{64,48},{80,64},{96,80},{112,96},{1... | collective-permute-start | bytes 884744 | tf_op jit(solution)/shard_map/piece_1_2/ppermute | solution.py:172
  63.5 6.0 %collective-permute-done.18.refs_2_ = f32[64,1152]{1,0:T(8,128)S(1)} collective-permute-done((f32[64,1152]{1,0:T(8,128)S(1)}, f32[64,1152]{1,0:T(8,128)S(1)}, u32[]{:S(2)}, u32[]{:S(2)}) %collective-permute-start.18) | collective-permute-done | bytes 294944 | tf_op jit(solution)/shard_map/piece_1_-2/ppermute | solution.py:172
  69.5 3.4 %collective-permute-start.19 = (f32[64,1152]{1,0:T(8,128)S(1)}, f32[64,1152]{1,0:T(8,128)S(1)}, u32[]{:S(2)}, u32[]{:S(2)}) collective-permute-start(f32[64,1152]{1,0:T(8,128)S(1)} %collective-permute-done.18.refs_2_), channel_id=1, source_target_pairs={{0,16},{16,32},{32,48},{48,64},{64,80},{80,96},{96,112},{112,0},{1... | collective-permute-start | bytes 884744 | tf_op jit(solution)/shard_map/piece_1_-3/ppermute | solution.py:172
  72.9 0.0 collective-permute-done.17.refs_3_
  72.9 3.8 %shard_map.50 = (f32[128,1152]{1,0:T(8,128)S(1)}, f32[128,1152]{1,0:T(8,128)S(1)}) custom-call(s32[18]{0:T(128)S(1)} %dynamic-slice_bitcast_fusion.table.flag, f32[64,1152]{1,0:T(8,128)S(1)} %collective-permute-done.13.refs_0_, f32[64,1152]{1,0:T(8,128)S(1)} %collective-permute-done.15.refs_1_, f32[64,1152]{1,0:T(8,128)S(1)} %collective-permute-done.16.refs_2_, ...), custom_call_target="tpu_custom_call" | custom-call | flops 2038431744 | bytes 7667712 | tf_op jit(solution)/shard_map/pallas_call | solution.py:239
  76.8 1.5 %collective-permute-start.24 = (f32[128,1152]{1,0:T(8,128)S(1)}, f32[128,1152]{1,0:T(8,128)S(1)}, u32[]{:S(2)}, u32[]{:S(2)}) collective-permute-start(f32[128,1152]{1,0:T(8,128)S(1)} %get-tuple-element.53), channel_id=1, source_target_pairs={{1,0},{2,1},{3,2},{4,3},{5,4},{6,5},{7,6},{8,7},{9,8},{10,9},{11,1... | collective-permute-start | bytes 1769480 | tf_op jit(solution)/shard_map/return_2/ppermute | solution.py:360
  78.3 0.0 collective-permute-done.22.refs_3_
  78.3 0.0 collective-permute-start.23
  78.3 0.0 collective-permute-done.19.refs_0_
  78.3 3.2 %collective-permute-start.25 = (f32[64,1152]{1,0:T(8,128)S(1)}, f32[64,1152]{1,0:T(8,128)S(1)}, u32[]{:S(2)}, u32[]{:S(2)}) collective-permute-start(f32[64,1152]{1,0:T(8,128)S(1)} %collective-permute-done.19.refs_0_), channel_id=1, source_target_pairs={{0,16},{16,32},{32,48},{48,64},{64,80},{80,96},{96,112},{112,0},{1... | collective-permute-start | bytes 884744 | tf_op jit(solution)/shard_map/piece_1_4/ppermute | solution.py:172
  81.6 0.0 collective-permute-done.20.refs_6_
  81.6 0.0 collective-permute-done.21.refs_1_
  81.6 3.8 %shard_map.51 = (f32[128,1152]{1,0:T(8,128)S(1)}, f32[128,1152]{1,0:T(8,128)S(1)}) custom-call(s32[18]{0:T(128)S(1)} %dynamic-slice_bitcast_fusion.table.flag, f32[64,1152]{1,0:T(8,128)S(1)} %collective-permute-done.19.refs_0_, f32[64,1152]{1,0:T(8,128)S(1)} %collective-permute-done.21.refs_1_, f32[64,1152]{1,0:T(8,128)S(1)} %collective-permute-done.18.refs_2_, ...), custom_call_target="tpu_custom_call" | custom-call | flops 2038431744 | bytes 7667712 | tf_op jit(solution)/shard_map/pallas_call | solution.py:239
  85.4 0.0 copy-start.1
  85.4 2.6 %collective-permute-start.26 = (f32[128,1152]{1,0:T(8,128)S(1)}, f32[128,1152]{1,0:T(8,128)S(1)}, u32[]{:S(2)}, u32[]{:S(2)}) collective-permute-start(f32[128,1152]{1,0:T(8,128)S(1)} %get-tuple-element.59), channel_id=1, source_target_pairs={{1,0},{2,1},{3,2},{4,3},{5,4},{6,5},{7,6},{8,7},{9,8},{10,9},{11,1... | collective-permute-start | bytes 1769480 | tf_op jit(solution)/shard_map/return_3/ppermute | solution.py:360
  88.0 0.9 collective-permute-done.23.refs_0_
  88.9 2.3 %shard_map.52 = (f32[64,1152]{1,0:T(8,128)S(1)}, f32[64,1152]{1,0:T(8,128)S(1)}) custom-call(s32[18]{0:T(128)S(1)} %dynamic-slice_bitcast_fusion.table.flag, f32[64,1152]{1,0:T(8,128)S(1)} %collective-permute-done.23.refs_0_, f32[64,1152]{1,0:T(8,128)S(1)} %collective-permute-done.25.refs_1_, bf16[1152,1152]{1,0:T(8,128)(2,1)S(1)} %get-tuple-element.43.refs_2_.refs_4_, ...), custom_call_target="tpu_custom_call" | custom-call | flops 1019215872 | bytes 6488064 | tf_op jit(solution)/shard_map/pallas_call | solution.py:239
  91.2 1.0 %collective-permute-start.27 = (f32[64,1152]{1,0:T(8,128)S(1)}, f32[64,1152]{1,0:T(8,128)S(1)}, u32[]{:S(2)}, u32[]{:S(2)}) collective-permute-start(f32[64,1152]{1,0:T(8,128)S(1)} %get-tuple-element.60), channel_id=1, source_target_pairs={{1,0},{2,1},{3,2},{4,3},{5,4},{6,5},{7,6},{8,7},{9,8},{10,9},{11,1... | collective-permute-start | bytes 884744 | tf_op jit(solution)/shard_map/return_4/ppermute | solution.py:360
  92.3 2.2 %shard_map.53.held = f32[512,1152]{1,0:T(8,128)S(1)} custom-call(s32[18]{0:T(128)S(1)} %dynamic-slice_bitcast_fusion.table.flag, f32[2]{0:T(128)S(1)} %pad_maximum_fusion.factors, f32[512,1152]{1,0:T(8,128)S(1)} %copy-done.1, f32[64,1152]{1,0:T(8,128)S(1)} %get-tuple-element.45.refs_0_, f32[128,1152]{1,0:T(8,128)S(1)} %get-tuple-element.46.refs_1_, ...), custom_call_target="tpu_custom_call" | custom-call | flops 2875392 | bytes 11501568 | tf_op jit(solution)/shard_map/pallas_call | solution.py:283
  94.4 5.7 %collective-permute-done.27.refs_1_ = f32[64,1152]{1,0:T(8,128)S(1)} collective-permute-done((f32[64,1152]{1,0:T(8,128)S(1)}, f32[64,1152]{1,0:T(8,128)S(1)}, u32[]{:S(2)}, u32[]{:S(2)}) %collective-permute-start.27) | collective-permute-done | bytes 294944 | tf_op jit(solution)/shard_map/return_4/ppermute | solution.py:360
  100.1 2.0 %shard_map.54 = f32[512,1152]{1,0:T(8,128)} custom-call(s32[18]{0:T(128)S(1)} %dynamic-slice_bitcast_fusion.table.flag, f32[2]{0:T(128)S(1)} %pad_maximum_fusion.factors, f32[512,1152]{1,0:T(8,128)S(1)} %shard_map.53.held, f32[128,1152]{1,0:T(8,128)S(1)} %collective-permute-done.26.refs_0_, f32[64,1152]{1,0:T(8,128)S(1)} %collective-permute-done.27.refs_1_), custom_call_target="tpu_custom_call" | custom-call | tf_op jit(solution)/shard_map/pallas_call | solution.py:322
  (9 shorter events, 0.0 us)
Async XLA Ops:
  0.0 1.7 %copy-start = (f32[512,1152]{1,0:T(8,128)S(1)}, f32[512,1152]{1,0:T(8,128)}, u32[]{:S(2)}) copy-start(f32[512,1152]{1,0:T(8,128)} %x.3) | copy-start | bytes 7077892
  2.2 7.4 %collective-permute-start.5 = (f32[128,1152]{1,0:T(8,128)S(1)}, f32[128,1152]{1,0:T(8,128)}, u32[]{:S(2)}, u32[]{:S(2)}) collective-permute-start(f32[128,1152]{1,0:T(8,128)S(1)} %get-tuple-element.38), channel_id=1, source_target_pairs={{0,4},{15,3},{17,19},{16,20},{34,38},{33,37},{51,177},{50,54},{68,... | collective-permute-start | bytes 1769480 | tf_op jit(solution)/shard_map/ppermute | solution.py:158
  3.7 6.6 %collective-permute-start.4 = (f32[128,1152]{1,0:T(8,128)S(1)}, f32[128,1152]{1,0:T(8,128)}, u32[]{:S(2)}, u32[]{:S(2)}) collective-permute-start(f32[128,1152]{1,0:T(8,128)S(1)} %get-tuple-element.37), channel_id=1, source_target_pairs={{0,128},{15,143},{17,29},{16,146},{34,162},{33,161},{51,63},{50,48... | collective-permute-start | bytes 1769480 | tf_op jit(solution)/shard_map/ppermute | solution.py:158
  5.2 7.0 %collective-permute-start = (f32[64,1152]{1,0:T(8,128)S(1)}, f32[64,1152]{1,0:T(8,128)S(1)}, u32[]{:S(2)}, u32[]{:S(2)}) collective-permute-start(f32[64,1152]{1,0:T(8,128)S(1)} %get-tuple-element.33), channel_id=1, source_target_pairs={{0,0},{15,112},{17,17},{16,1},{34,34},{33,18},{51,51},{50,35},{68,... | collective-permute-start | bytes 884744 | tf_op jit(solution)/shard_map/ppermute | solution.py:159
  5.9 14.6 %collective-permute-start.1 = (f32[64,1152]{1,0:T(8,128)S(1)}, f32[64,1152]{1,0:T(8,128)S(1)}, u32[]{:S(2)}, u32[]{:S(2)}) collective-permute-start(f32[64,1152]{1,0:T(8,128)S(1)} %get-tuple-element.34), channel_id=1, source_target_pairs={{0,208},{15,48},{17,81},{16,177},{34,242},{33,82},{51,115},{50,211... | collective-permute-start | bytes 884744 | tf_op jit(solution)/shard_map/ppermute | solution.py:159
  7.2 13.3 %collective-permute-start.2 = (f32[64,1152]{1,0:T(8,128)S(1)}, f32[64,1152]{1,0:T(8,128)S(1)}, u32[]{:S(2)}, u32[]{:S(2)}) collective-permute-start(f32[64,1152]{1,0:T(8,128)S(1)} %get-tuple-element.35), channel_id=1, source_target_pairs={{0,64},{15,192},{17,161},{16,209},{34,98},{33,226},{51,195},{50,24... | collective-permute-start | bytes 884744 | tf_op jit(solution)/shard_map/ppermute | solution.py:159
  9.6 11.0 %collective-permute-start.3 = (f32[64,1152]{1,0:T(8,128)S(1)}, f32[64,1152]{1,0:T(8,128)S(1)}, u32[]{:S(2)}, u32[]{:S(2)}) collective-permute-start(f32[64,1152]{1,0:T(8,128)S(1)} %get-tuple-element.36), channel_id=1, source_target_pairs={{0,32},{15,224},{17,225},{16,65},{34,66},{33,130},{51,131},{50,99}... | collective-permute-start | bytes 884744 | tf_op jit(solution)/shard_map/ppermute | solution.py:159
  11.6 9.0 %collective-permute-start.6 = (f32[64,1152]{1,0:T(8,128)S(1)}, f32[64,1152]{1,0:T(8,128)S(1)}, u32[]{:S(2)}, u32[]{:S(2)}) collective-permute-start(f32[64,1152]{1,0:T(8,128)S(1)} %get-tuple-element.64), channel_id=1, source_target_pairs={{128,144},{4,176},{143,160},{3,128},{29,129},{19,113},{146,33},{20... | collective-permute-start | bytes 884744 | tf_op jit(solution)/shard_map/ppermute | solution.py:161
  12.3 8.3 %collective-permute-start.7 = (f32[64,1152]{1,0:T(8,128)S(1)}, f32[64,1152]{1,0:T(8,128)S(1)}, u32[]{:S(2)}, u32[]{:S(2)}) collective-permute-start(f32[64,1152]{1,0:T(8,128)S(1)} %get-tuple-element.63), channel_id=1, source_target_pairs={{128,96},{4,240},{143,80},{3,16},{29,193},{19,49},{146,241},{20,14... | collective-permute-start | bytes 884744 | tf_op jit(solution)/shard_map/ppermute | solution.py:161
  21.2 15.6 %collective-permute-start.8 = (f32[64,1152]{1,0:T(8,128)S(1)}, f32[64,1152]{1,0:T(8,128)S(1)}, u32[]{:S(2)}, u32[]{:S(2)}) collective-permute-start(f32[64,1152]{1,0:T(8,128)S(1)} %shard_map.47.refs_0_), channel_id=1, source_target_pairs={{0,112},{16,0},{32,16},{48,32},{64,48},{80,64},{96,80},{112,96},{1... | collective-permute-start | bytes 884744 | tf_op jit(solution)/shard_map/piece_0_1/ppermute | solution.py:172
  32.7 7.2 %collective-permute-start.10 = (f32[64,1152]{1,0:T(8,128)S(1)}, f32[64,1152]{1,0:T(8,128)S(1)}, u32[]{:S(2)}, u32[]{:S(2)}) collective-permute-start(f32[64,1152]{1,0:T(8,128)S(1)} %shard_map.47.refs_0_), channel_id=1, source_target_pairs={{0,16},{16,32},{32,48},{48,64},{64,80},{80,96},{96,112},{112,0},{1... | collective-permute-start | bytes 884744 | tf_op jit(solution)/shard_map/piece_0_-1/ppermute | solution.py:172
  32.7 12.5 %collective-permute-start.12 = (f32[64,1152]{1,0:T(8,128)S(1)}, f32[64,1152]{1,0:T(8,128)S(1)}, u32[]{:S(2)}, u32[]{:S(2)}) collective-permute-start(f32[64,1152]{1,0:T(8,128)S(1)} %shard_map.47.refs_0_), channel_id=1, source_target_pairs={{0,128},{16,144},{32,160},{48,176},{64,192},{80,208},{96,224},{112... | collective-permute-start | bytes 884744 | tf_op jit(solution)/shard_map/piece_1_0/ppermute | solution.py:172
  36.8 17.6 %collective-permute-start.9 = (f32[64,1152]{1,0:T(8,128)S(1)}, f32[64,1152]{1,0:T(8,128)S(1)}, u32[]{:S(2)}, u32[]{:S(2)}) collective-permute-start(f32[64,1152]{1,0:T(8,128)S(1)} %collective-permute-done.8.refs_1_), channel_id=1, source_target_pairs={{0,112},{16,0},{32,16},{48,32},{64,48},{80,64},{96,80},{112,96},{1... | collective-permute-start | bytes 884744 | tf_op jit(solution)/shard_map/piece_0_2/ppermute | solution.py:172
  39.9 14.5 %collective-permute-start.11 = (f32[64,1152]{1,0:T(8,128)S(1)}, f32[64,1152]{1,0:T(8,128)S(1)}, u32[]{:S(2)}, u32[]{:S(2)}) collective-permute-start(f32[64,1152]{1,0:T(8,128)S(1)} %collective-permute-done.10.refs_2_), channel_id=1, source_target_pairs={{0,16},{16,32},{32,48},{48,64},{64,80},{80,96},{96,112},{112,0},{1... | collective-permute-start | bytes 884744 | tf_op jit(solution)/shard_map/piece_0_-2/ppermute | solution.py:172
  39.9 17.2 %collective-permute-start.15 = (f32[64,1152]{1,0:T(8,128)S(1)}, f32[64,1152]{1,0:T(8,128)S(1)}, u32[]{:S(2)}, u32[]{:S(2)}) collective-permute-start(f32[64,1152]{1,0:T(8,128)S(1)} %collective-permute-done.10.refs_2_), channel_id=1, source_target_pairs={{0,128},{16,144},{32,160},{48,176},{64,192},{80,208},{96,224},{112... | collective-permute-start | bytes 884744 | tf_op jit(solution)/shard_map/piece_1_-1/ppermute | solution.py:172
  42.6 18.7 %collective-permute-start.13 = (f32[64,1152]{1,0:T(8,128)S(1)}, f32[64,1152]{1,0:T(8,128)S(1)}, u32[]{:S(2)}, u32[]{:S(2)}) collective-permute-start(f32[64,1152]{1,0:T(8,128)S(1)} %collective-permute-done.8.refs_1_), channel_id=1, source_target_pairs={{0,128},{16,144},{32,160},{48,176},{64,192},{80,208},{96,224},{112... | collective-permute-start | bytes 884744 | tf_op jit(solution)/shard_map/piece_1_1/ppermute | solution.py:172
  45.2 16.8 %collective-permute-start.14 = (f32[64,1152]{1,0:T(8,128)S(1)}, f32[64,1152]{1,0:T(8,128)S(1)}, u32[]{:S(2)}, u32[]{:S(2)}) collective-permute-start(f32[64,1152]{1,0:T(8,128)S(1)} %get-tuple-element.47), channel_id=1, source_target_pairs={{1,0},{2,1},{3,2},{4,3},{5,4},{6,5},{7,6},{8,7},{9,8},{10,9},{11,1... | collective-permute-start | bytes 884744 | tf_op jit(solution)/shard_map/return_0/ppermute | solution.py:360
  54.4 18.5 %collective-permute-start.16 = (f32[64,1152]{1,0:T(8,128)S(1)}, f32[64,1152]{1,0:T(8,128)S(1)}, u32[]{:S(2)}, u32[]{:S(2)}) collective-permute-start(f32[64,1152]{1,0:T(8,128)S(1)} %collective-permute-done.9.refs_0_), channel_id=1, source_target_pairs={{0,112},{16,0},{32,16},{48,32},{64,48},{80,64},{96,80},{112,96},{1... | collective-permute-start | bytes 884744 | tf_op jit(solution)/shard_map/piece_0_3/ppermute | solution.py:172
  54.4 18.5 %collective-permute-start.17 = (f32[64,1152]{1,0:T(8,128)S(1)}, f32[64,1152]{1,0:T(8,128)S(1)}, u32[]{:S(2)}, u32[]{:S(2)}) collective-permute-start(f32[64,1152]{1,0:T(8,128)S(1)} %collective-permute-done.11.refs_1_), channel_id=1, source_target_pairs={{0,16},{16,32},{32,48},{48,64},{64,80},{80,96},{96,112},{112,0},{1... | collective-permute-start | bytes 884744 | tf_op jit(solution)/shard_map/piece_0_-3/ppermute | solution.py:172
  57.1 12.3 %collective-permute-start.18 = (f32[64,1152]{1,0:T(8,128)S(1)}, f32[64,1152]{1,0:T(8,128)S(1)}, u32[]{:S(2)}, u32[]{:S(2)}) collective-permute-start(f32[64,1152]{1,0:T(8,128)S(1)} %collective-permute-done.15.refs_1_), channel_id=1, source_target_pairs={{0,16},{16,32},{32,48},{48,64},{64,80},{80,96},{96,112},{112,0},{1... | collective-permute-start | bytes 884744 | tf_op jit(solution)/shard_map/piece_1_-2/ppermute | solution.py:172
  61.3 20.3 %collective-permute-start.20 = (f32[128,1152]{1,0:T(8,128)S(1)}, f32[128,1152]{1,0:T(8,128)S(1)}, u32[]{:S(2)}, u32[]{:S(2)}) collective-permute-start(f32[128,1152]{1,0:T(8,128)S(1)} %get-tuple-element.50), channel_id=1, source_target_pairs={{1,0},{2,1},{3,2},{4,3},{5,4},{6,5},{7,6},{8,7},{9,8},{10,9},{11,1... | collective-permute-start | bytes 1769480 | tf_op jit(solution)/shard_map/return_1/ppermute | solution.py:360
  62.0 16.3 %collective-permute-start.22 = (f32[64,1152]{1,0:T(8,128)S(1)}, f32[64,1152]{1,0:T(8,128)S(1)}, u32[]{:S(2)}, u32[]{:S(2)}) collective-permute-start(f32[64,1152]{1,0:T(8,128)S(1)} %collective-permute-done.13.refs_0_), channel_id=1, source_target_pairs={{0,112},{16,0},{32,16},{48,32},{64,48},{80,64},{96,80},{112,96},{1... | collective-permute-start | bytes 884744 | tf_op jit(solution)/shard_map/piece_1_2/ppermute | solution.py:172
  69.5 8.8 %collective-permute-start.19 = (f32[64,1152]{1,0:T(8,128)S(1)}, f32[64,1152]{1,0:T(8,128)S(1)}, u32[]{:S(2)}, u32[]{:S(2)}) collective-permute-start(f32[64,1152]{1,0:T(8,128)S(1)} %collective-permute-done.18.refs_2_), channel_id=1, source_target_pairs={{0,16},{16,32},{32,48},{48,64},{64,80},{80,96},{96,112},{112,0},{1... | collective-permute-start | bytes 884744 | tf_op jit(solution)/shard_map/piece_1_-3/ppermute | solution.py:172
  72.9 8.7 %collective-permute-start.21 = (f32[64,1152]{1,0:T(8,128)S(1)}, f32[64,1152]{1,0:T(8,128)S(1)}, u32[]{:S(2)}, u32[]{:S(2)}) collective-permute-start(f32[64,1152]{1,0:T(8,128)S(1)} %collective-permute-done.16.refs_2_), channel_id=1, source_target_pairs={{0,112},{16,0},{32,16},{48,32},{64,48},{80,64},{96,80},{112,96},{1... | collective-permute-start | bytes 884744 | tf_op jit(solution)/shard_map/piece_0_4/ppermute | solution.py:172
  76.8 12.1 %collective-permute-start.24 = (f32[128,1152]{1,0:T(8,128)S(1)}, f32[128,1152]{1,0:T(8,128)S(1)}, u32[]{:S(2)}, u32[]{:S(2)}) collective-permute-start(f32[128,1152]{1,0:T(8,128)S(1)} %get-tuple-element.53), channel_id=1, source_target_pairs={{1,0},{2,1},{3,2},{4,3},{5,4},{6,5},{7,6},{8,7},{9,8},{10,9},{11,1... | collective-permute-start | bytes 1769480 | tf_op jit(solution)/shard_map/return_2/ppermute | solution.py:360
  78.3 10.6 %collective-permute-start.23 = (f32[64,1152]{1,0:T(8,128)S(1)}, f32[64,1152]{1,0:T(8,128)S(1)}, u32[]{:S(2)}, u32[]{:S(2)}) collective-permute-start(f32[64,1152]{1,0:T(8,128)S(1)} %collective-permute-done.22.refs_3_), channel_id=1, source_target_pairs={{0,112},{16,0},{32,16},{48,32},{64,48},{80,64},{96,80},{112,96},{1... | collective-permute-start | bytes 884744 | tf_op jit(solution)/shard_map/piece_1_3/ppermute | solution.py:172
  78.3 10.6 %collective-permute-start.25 = (f32[64,1152]{1,0:T(8,128)S(1)}, f32[64,1152]{1,0:T(8,128)S(1)}, u32[]{:S(2)}, u32[]{:S(2)}) collective-permute-start(f32[64,1152]{1,0:T(8,128)S(1)} %collective-permute-done.19.refs_0_), channel_id=1, source_target_pairs={{0,16},{16,32},{32,48},{48,64},{64,80},{80,96},{96,112},{112,0},{1... | collective-permute-start | bytes 884744 | tf_op jit(solution)/shard_map/piece_1_4/ppermute | solution.py:172
  85.4 6.8 %copy-start.1 = (f32[512,1152]{1,0:T(8,128)S(1)}, f32[512,1152]{1,0:T(8,128)}, u32[]{:S(2)}) copy-start(f32[512,1152]{1,0:T(8,128)} %x.3) | copy-start | bytes 7077892
  85.4 14.7 %collective-permute-start.26 = (f32[128,1152]{1,0:T(8,128)S(1)}, f32[128,1152]{1,0:T(8,128)S(1)}, u32[]{:S(2)}, u32[]{:S(2)}) collective-permute-start(f32[128,1152]{1,0:T(8,128)S(1)} %get-tuple-element.59), channel_id=1, source_target_pairs={{1,0},{2,1},{3,2},{4,3},{5,4},{6,5},{7,6},{8,7},{9,8},{10,9},{11,1... | collective-permute-start | bytes 1769480 | tf_op jit(solution)/shard_map/return_3/ppermute | solution.py:360
  91.2 8.9 %collective-permute-start.27 = (f32[64,1152]{1,0:T(8,128)S(1)}, f32[64,1152]{1,0:T(8,128)S(1)}, u32[]{:S(2)}, u32[]{:S(2)}) collective-permute-start(f32[64,1152]{1,0:T(8,128)S(1)} %get-tuple-element.60), channel_id=1, source_target_pairs={{1,0},{2,1},{3,2},{4,3},{5,4},{6,5},{7,6},{8,7},{9,8},{10,9},{11,1... | collective-permute-start | bytes 884744 | tf_op jit(solution)/shard_map/return_4/ppermute | solution.py:360
